TPU v7x, 32 devices: a whole 2x2x4 slice. The times are simulated.
32 devices in a mesh: section: 2 (over x), tensor: 4 (over y, core), dp: 4 (over z).
Axes of the slice: x: 2, y: 2, z: 4, core: 2. Of those that a mesh axis runs over, the one named last changes fastest.
Arguments:
- images: bfloat16 [8, 256, 1152], P('dp', 'tensor'), may hold values from -6 to 6
- timesteps: int32 [8], P('dp'), may hold values from 0 to 999
- t_table: bfloat16 [1000, 1152], replicated, may hold values from -6 to 6
- rel_index: int32 [256, 256], replicated, may hold values from 0 to 960, as said below
- w_qkv: bfloat16 [2, 1152, 3, 1152], P('section', None, None, 'tensor'), may hold values from -0.1875 to 0.1875
- w_time: bfloat16 [2, 1152, 3, 1152], P('section', None, None, 'tensor'), may hold values from -0.1875 to 0.1875
- w_out: bfloat16 [2, 1152, 1152], P('section', 'tensor'), may hold values from -0.5 to 0.5
- w_fc1: bfloat16 [2, 1152, 4608], P('section', None, 'tensor'), may hold values from -0.1875 to 0.1875
- w_fc2: bfloat16 [2, 4608, 1152], P('section', 'tensor'), may hold values from -0.09375 to 0.09375
- rel_table: float32 [2, 961, 16], P('section', None, 'tensor'), may hold values from -4 to 4
- norm_gain: float32 [2, 2, 1152], P('section'), may hold values from 0.1 to 1.9
- norm_shift: float32 [2, 2, 1152], P('section'), may hold values from -2 to 2
- cotangent: bfloat16 [8, 256, 1152], P('dp', 'tensor'), may hold values from -6 to 6
Outputs:
- output: bfloat16 [8, 256, 1152], P('dp', 'tensor')
- input_grads: bfloat16 [2, 8, 256, 1152], P('section', 'dp', 'tensor')
- g_qkv: float32 [2, 1152, 3, 1152], P('section', 'dp', None, 'tensor')
- g_time: float32 [2, 1152, 3, 1152], P('section', 'dp', None, 'tensor')
- g_out: float32 [2, 1152, 1152], P('section', 'tensor', 'dp')
- g_fc1: float32 [2, 1152, 4608], P('section', 'dp', 'tensor')
- g_fc2: float32 [2, 4608, 1152], P('section', 'tensor', 'dp')
- g_table: float32 [2, 961, 16], P('section', None, 'tensor')
- g_gain: float32 [2, 2, 1152], P('section')
- g_shift: float32 [2, 2, 1152], P('section')
Inputs may be any that keep to these rules, and one draw needn't show every extreme that they name: `rel_index`: tokens at the same offset between rows and between columns of the patch grid share a bucket; every bucket is used.
All inputs are finite; a program needn't handle non-finite values.
Results may differ from a plain program's by a relative error of at most 0.02.
Values may be sent and summed in bfloat16 or wider, within the bound.
A program may use at most 256 MiB of HBM per device.

v0:
```python
import jax
import jax.numpy as jnp
from jax import lax
from jax.sharding import PartitionSpec as P

MICRO = 2


norm_eps = 1e-06


def from_behind(x, axis, by):
    length = lax.axis_size(axis)
    return lax.ppermute(x, axis, [(i, (i + by) % length) for i in range(length)])


def from_behind_2(block, axis, distance):
    devices = range(lax.axis_size(axis))
    route = [(i - distance, i) for i in devices if i - distance in devices]
    return lax.ppermute(block, axis, route)


def layer_norm(rows, gain, shift):
    centre = rows - jnp.mean(rows, axis=-1, keepdims=True)
    spread = jnp.mean(centre * centre, axis=-1, keepdims=True)
    return centre * lax.rsqrt(spread + norm_eps) * gain + shift


def gelu_tanh(values):
    return jax.nn.gelu(values, approximate=True)


def gather_rows(rows):
    return lax.all_gather(rows, "tensor", axis=1, tiled=True)


def sum_rows(terms):
    return lax.psum_scatter(
        terms.astype(jnp.bfloat16), "tensor", scatter_dimension=1, tiled=True
    ).astype(jnp.float32)


def gather_grads(rows):
    return lax.all_gather(rows, "tensor", axis=1, tiled=True)


def sum_grads(terms):
    return lax.psum_scatter(
        terms.astype(jnp.bfloat16), "tensor", scatter_dimension=1, tiled=True
    ).astype(jnp.float32)


def split_heads(qkv, heads):
    count, seq, _, local = qkv.shape
    width = local // heads
    query = qkv[:, :, 0].reshape(count, seq, heads, width)
    keys = qkv[:, :, 1].reshape(count, seq, heads, width)
    values = qkv[:, :, 2].reshape(count, seq, heads, width)
    return (query, keys, values, width ** (-0.5))


def head_scores(query, keys, bias_heads, scale):
    return (
        jnp.einsum("iqhe,ikhe->ihqk", query, keys, preferred_element_type=jnp.float32) * scale
        + bias_heads[None]
    )


def forward_block(x_rows, time_part, weights, bias_heads):
    w_qkv, w_out, w_fc1, w_fc2, gains, shifts = weights
    a_first = layer_norm(x_rows, gains[0], shifts[0]).astype(jnp.bfloat16)
    a_whole = gather_rows(a_first)
    qkv = (
        jnp.einsum("isd,dcj->iscj", a_whole, w_qkv, preferred_element_type=jnp.float32)
        + time_part[:, None]
    )
    qkv = qkv.astype(jnp.bfloat16)
    count, seq, _, local = qkv.shape
    query, keys, values, scale = split_heads(qkv, bias_heads.shape[0])
    scores = head_scores(query, keys, bias_heads, scale)
    top = jnp.max(scores, axis=-1, keepdims=True)
    expo = jnp.exp(scores - top)
    total = jnp.sum(expo, axis=-1, keepdims=True)
    probs = (expo / total).astype(jnp.bfloat16)
    log_total = top + jnp.log(total)
    attended = jnp.einsum("ihqk,ikhe->iqhe", probs, values, preferred_element_type=jnp.float32)
    attended = attended.reshape(count, seq, local).astype(jnp.bfloat16)
    branch = sum_rows(
        jnp.einsum("isj,jd->isd", attended, w_out, preferred_element_type=jnp.float32)
    )
    y_mid = x_rows + branch
    a_second = layer_norm(y_mid, gains[1], shifts[1]).astype(jnp.bfloat16)
    a_whole2 = gather_rows(a_second)
    hidden = jnp.einsum("isd,df->isf", a_whole2, w_fc1, preferred_element_type=jnp.float32)
    active = gelu_tanh(hidden).astype(jnp.bfloat16)
    mixed = sum_rows(jnp.einsum("isf,fd->isd", active, w_fc2, preferred_element_type=jnp.float32))
    return (y_mid + mixed, (a_whole, qkv, log_total, attended, y_mid, a_whole2, hidden, active))


def input_part(grad_out, x_rows, tvec, cache, weights, bias_heads, rel_index):
    w_qkv, w_out, w_fc1, w_fc2, gains, shifts = weights
    a_whole, qkv, log_total, attended, y_mid, a_whole2, hidden, active = cache
    grad_mlp = gather_grads(grad_out.astype(jnp.bfloat16))
    grad_active = jnp.einsum("isd,fd->isf", grad_mlp, w_fc2, preferred_element_type=jnp.float32)
    gelu_back = jax.vjp(gelu_tanh, hidden)[1]
    grad_hidden = gelu_back(grad_active)[0].astype(jnp.bfloat16)
    grad_norm2 = sum_grads(
        jnp.einsum("isf,df->isd", grad_hidden, w_fc1, preferred_element_type=jnp.float32)
    )
    norm_back2 = jax.vjp(layer_norm, y_mid, gains[1], shifts[1])[1]
    grad_ln2, g_gain2, g_shift2 = norm_back2(grad_norm2)
    grad_ymid = grad_out + grad_ln2
    grad_branch = gather_grads(grad_ymid.astype(jnp.bfloat16))
    grad_att = jnp.einsum(
        "isd,jd->isj", grad_branch, w_out, preferred_element_type=jnp.float32
    ).astype(jnp.bfloat16)
    count, seq, _, local = qkv.shape
    heads = bias_heads.shape[0]
    query, keys, values, scale = split_heads(qkv, heads)
    grad_att = grad_att.reshape(count, seq, heads, local // heads)
    scores = head_scores(query, keys, bias_heads, scale)
    probs = jnp.exp(scores - log_total)
    grad_probs = jnp.einsum("iqhe,ikhe->ihqk", grad_att, values, preferred_element_type=jnp.float32)
    inner = jnp.sum(probs * grad_probs, axis=-1, keepdims=True)
    grad_scores = (probs * (grad_probs - inner)).astype(jnp.bfloat16)
    grad_query = (
        jnp.einsum("ihqk,ikhe->iqhe", grad_scores, keys, preferred_element_type=jnp.float32) * scale
    )
    grad_keys = (
        jnp.einsum("ihqk,iqhe->ikhe", grad_scores, query, preferred_element_type=jnp.float32)
        * scale
    )
    grad_values = jnp.einsum(
        "ihqk,iqhe->ikhe", probs.astype(jnp.bfloat16), grad_att, preferred_element_type=jnp.float32
    )
    grad_qkv = jnp.stack(
        [
            grad_query.reshape(count, seq, local),
            grad_keys.reshape(count, seq, local),
            grad_values.reshape(count, seq, local),
        ],
        axis=2,
    ).astype(jnp.bfloat16)
    flat_scores = jnp.sum(grad_scores.astype(jnp.float32), axis=0).reshape(heads, seq * seq).T
    g_table = jax.ops.segment_sum(
        flat_scores, rel_index.reshape(-1), num_segments=(2 * int(round(seq**0.5)) - 1) ** 2
    )
    grad_norm1 = sum_grads(
        jnp.einsum("iscj,dcj->isd", grad_qkv, w_qkv, preferred_element_type=jnp.float32)
    )
    norm_back1 = jax.vjp(layer_norm, x_rows, gains[0], shifts[0])[1]
    grad_ln1, g_gain1, g_shift1 = norm_back1(grad_norm1)
    grad_x = grad_ymid + grad_ln1
    small_terms = (
        g_table[None],
        jnp.stack([g_gain1, g_gain2])[None],
        jnp.stack([g_shift1, g_shift2])[None],
    )
    operands = (
        active,
        grad_mlp,
        a_whole2,
        grad_hidden,
        attended,
        grad_branch,
        a_whole,
        grad_qkv,
        tvec,
    )
    return (grad_x, small_terms, operands)


def weight_part(operands):
    active, grad_mlp, a_whole2, grad_hidden, attended, grad_branch, a_whole, grad_qkv, tvec = (
        operands
    )
    g_fc2 = jnp.einsum("isf,isd->fd", active, grad_mlp, preferred_element_type=jnp.float32)
    g_fc1 = jnp.einsum("isd,isf->df", a_whole2, grad_hidden, preferred_element_type=jnp.float32)
    g_out = jnp.einsum("isj,isd->jd", attended, grad_branch, preferred_element_type=jnp.float32)
    g_qkv = jnp.einsum("isd,iscj->dcj", a_whole, grad_qkv, preferred_element_type=jnp.float32)
    token_sums = jnp.sum(grad_qkv.astype(jnp.float32), axis=1)
    g_time = jnp.einsum(
        "id,icj->dcj", tvec.astype(jnp.float32), token_sums, precision=lax.Precision.HIGHEST
    )
    return (g_qkv[None], g_time[None], g_out[None], g_fc1[None], g_fc2[None])


def settle(operands):
    weight_terms = weight_part(operands)
    return tuple(weight_terms)


def add_terms(total, terms):
    if total is None:
        return terms
    return jax.tree.map(lambda left, right: left + right, total, terms)


def per_device(
    images,
    timesteps,
    t_table,
    rel_index,
    w_qkv,
    w_time,
    w_out,
    w_fc1,
    w_fc2,
    rel_table,
    norm_gain,
    norm_shift,
    cotangent,
):
    first = lax.axis_index("section") == 0
    per = images.shape[0] // MICRO
    embedded = t_table[timesteps]
    weights = (w_qkv[0], w_out[0], w_fc1[0], w_fc2[0], norm_gain[0], norm_shift[0])
    bias_heads = jnp.transpose(rel_table[0][rel_index], (2, 0, 1))
    time_all = jnp.einsum("id,dcj->icj", embedded, w_time[0], preferred_element_type=jnp.float32)

    def pick(array, micro):
        return array[micro * per : (micro + 1) * per]

    received = jnp.zeros_like(pick(images, 0))
    inputs, tvecs, times, caches, outputs = ([], [], [], [], [])
    for tick in range(MICRO + 1):
        own = min(tick, MICRO - 1)
        before = max(tick - 1, 0)
        block_in = jnp.where(first, pick(images, own), received)
        tvec = jnp.where(first, pick(embedded, own), pick(embedded, before))
        time_part = jnp.where(first, pick(time_all, own), pick(time_all, before))
        result, cache = forward_block(block_in.astype(jnp.float32), time_part, weights, bias_heads)
        sent = result.astype(jnp.bfloat16)
        received = from_behind(sent, "section", 1)
        inputs.append(block_in)
        tvecs.append(tvec)
        times.append(time_part)
        if tick >= 1:
            outputs.append(jnp.where(first, received, sent))
    back_in = jnp.zeros_like(pick(cotangent, 0))
    weight_total = None
    small_total = None
    sent_grads = []
    for tick in range(MICRO + 1):
        lower = max(tick - 1, 0)
        upper = min(tick + 1, MICRO)
        valid = jnp.where(first, tick >= 1, tick < MICRO)
        grad_in = jnp.where(first, back_in, pick(cotangent, min(tick, MICRO - 1)))
        grad_in = jnp.where(valid, grad_in, jnp.zeros_like(grad_in))
        x_rows = jnp.where(first, inputs[lower], inputs[upper]).astype(jnp.float32)
        tvec = jnp.where(first, tvecs[lower], tvecs[upper])
        time_part = jnp.where(first, times[lower], times[upper])
        cache = forward_block(x_rows, time_part, weights, bias_heads)[1]
        grad_x, small_terms, operands = input_part(
            grad_in.astype(jnp.float32), x_rows, tvec, cache, weights, bias_heads, rel_index
        )
        small_total = add_terms(small_total, small_terms)
        grad_sent = grad_x.astype(jnp.bfloat16)
        back_in = from_behind_2(grad_sent, "section", -1)
        weight_total = add_terms(weight_total, settle(operands))
        sent_grads.append(grad_sent)
    weight_total = (
        lax.psum_scatter(
            weight_total[0].astype(jnp.bfloat16), "dp", scatter_dimension=1, tiled=True
        ).astype(jnp.float32),
        lax.psum_scatter(
            weight_total[1].astype(jnp.bfloat16), "dp", scatter_dimension=1, tiled=True
        ).astype(jnp.float32),
        lax.psum_scatter(
            weight_total[2].astype(jnp.bfloat16), "dp", scatter_dimension=2, tiled=True
        ).astype(jnp.float32),
        lax.psum_scatter(
            weight_total[3].astype(jnp.bfloat16), "dp", scatter_dimension=1, tiled=True
        ).astype(jnp.float32),
        lax.psum_scatter(
            weight_total[4].astype(jnp.bfloat16), "dp", scatter_dimension=2, tiled=True
        ).astype(jnp.float32),
    )
    g_qkv, g_time, g_out, g_fc1, g_fc2 = weight_total
    g_table = lax.psum(small_total[0], "dp")
    g_gain, g_shift = lax.psum((small_total[1], small_total[2]), ("tensor", "dp"))
    output = jnp.concatenate(outputs, axis=0)
    own_grads = [
        jnp.where(first, sent_grads[tick], sent_grads[tick - 1]) for tick in range(1, MICRO + 1)
    ]
    input_grads = jnp.concatenate(own_grads, axis=0)[None]
    return (output, input_grads, g_qkv, g_time, g_out, g_fc1, g_fc2, g_table, g_gain, g_shift)


def solution(mesh):
    in_specs = (
        P("dp", "tensor", None),
        P("dp"),
        P(),
        P(),
        P("section", None, None, "tensor"),
        P("section", None, None, "tensor"),
        P("section", "tensor", None),
        P("section", None, "tensor"),
        P("section", "tensor", None),
        P("section", None, "tensor"),
        P("section", None, None),
        P("section", None, None),
        P("dp", "tensor", None),
    )
    out_specs = (
        P("dp", "tensor", None),
        P("section", "dp", "tensor", None),
        P("section", "dp", None, "tensor"),
        P("section", "dp", None, "tensor"),
        P("section", "tensor", "dp"),
        P("section", "dp", "tensor"),
        P("section", "tensor", "dp"),
        P("section", None, "tensor"),
        P("section", None, None),
        P("section", None, None),
    )
    return jax.shard_map(
        per_device, mesh=mesh, in_specs=in_specs, out_specs=out_specs, check_vma=False
    )
```

profile of v0, /device:TPU:9, one launch (start us, length us, event | category | flops | bytes accessed | tf_op | source)
XLA Modules:
  0.0 2120.7 jit_solution(5378373442058326400)
XLA Ops:
  11.5 8.1 all_gather.54
  28.1 236.4 %gather_fusion.1 = f32[65536,4]{1,0:T(8,128)} fusion(f32[961,4]{1,0:T(8,128)S(1)} %bitcast.553, s32[65536]{0:T(1024)} %broadcast_clamp_fusion), kind=kCustom, calls=%fused_computation.1 | custom fusion | bytes 2359296 | tf_op jit(solution)/shard_map/gather | solution.py:218
  264.5 19.8 copy.71
  290.3 22.4 %reduce-scatter.27.cloned.1.call-done = bf16[1,64,1152]{2,1,0:T(8,128)(2,1)} async-done(((bf16[1,256,1152]{2,1,0:T(8,128)(2,1)}), bf16[1,64,1152]{2,1,0:T(8,128)(2,1)}) %reduce-scatter.27.cloned.1.call-update) | async-done | bytes 147472 | tf_op jit(solution)/shard_map/reduce_scatter | solution.py:38
  316.2 8.1 all_gather.55
  324.3 4.6 fusion.78
  329.0 22.0 %reduce-scatter.29.cloned.1.call-done = bf16[1,64,1152]{2,1,0:T(8,128)(2,1)} async-done(((bf16[1,256,1152]{2,1,0:T(8,128)(2,1)}), bf16[1,64,1152]{2,1,0:T(8,128)(2,1)}) %reduce-scatter.29.cloned.1.call-update) | async-done | bytes 147472 | tf_op jit(solution)/shard_map/reduce_scatter | solution.py:38
  358.5 8.1 all_gather.56
  374.7 22.5 %reduce-scatter.31.cloned.1.call-done = bf16[1,64,1152]{2,1,0:T(8,128)(2,1)} async-done(((bf16[1,256,1152]{2,1,0:T(8,128)(2,1)}), bf16[1,64,1152]{2,1,0:T(8,128)(2,1)}) %reduce-scatter.31.cloned.1.call-update) | async-done | bytes 147472 | tf_op jit(solution)/shard_map/reduce_scatter | solution.py:38
  400.6 8.1 all_gather.57
  408.7 4.6 fusion.75
  414.9 8.3 all_gather.60
  423.4 12.0 reduce-scatter.33.cloned.1.call-done
  444.7 8.1 all_gather.69
  457.7 7.9 all_gather.58
  475.3 9.5 all_gather.61
  492.3 14.2 reduce-scatter.35.cloned.1.call-done
  510.5 20.6 reduce-scatter.39.cloned.1.call-done
  536.1 8.1 all_gather.59
  544.2 4.6 fusion.72
  548.9 8.1 all_gather.62
  563.7 7.2 reduce-scatter.37.cloned.1.call-done
  573.5 7.6 all_gather.65
  586.0 9.5 reduce-scatter.41.cloned.1.call-done
  597.4 23.2 %reduce-scatter.45.cloned.1.call-done = bf16[1,64,1152]{2,1,0:T(8,128)(2,1)} async-done(((bf16[1,256,1152]{2,1,0:T(8,128)(2,1)}), bf16[1,64,1152]{2,1,0:T(8,128)(2,1)}) %reduce-scatter.45.cloned.1.call-update) | async-done | bytes 147472 | tf_op jit(solution)/shard_map/reduce_scatter | solution.py:38
  625.3 7.8 all_gather.63
  639.7 9.1 all_gather.66
  648.8 13.0 reduce-scatter.43.cloned.1.call-done
  673.2 8.5 all_gather.64
  685.6 21.6 %reduce-scatter.47.cloned.1.call-done = bf16[1,64,1152]{2,1,0:T(8,128)(2,1)} async-done(((bf16[1,256,1152]{2,1,0:T(8,128)(2,1)}), bf16[1,64,1152]{2,1,0:T(8,128)(2,1)}) %reduce-scatter.47.cloned.1.call-update) | async-done | bytes 147472 | tf_op jit(solution)/shard_map/reduce_scatter | solution.py:48
  711.3 7.8 all_gather.67
  725.5 9.1 all_gather.70
  734.6 13.1 reduce-scatter.49.cloned.1.call-done
  761.4 8.1 all_gather.68
  773.5 21.6 %reduce-scatter.53.cloned.1.call-done = bf16[1,64,1152]{2,1,0:T(8,128)(2,1)} async-done(((bf16[1,256,1152]{2,1,0:T(8,128)(2,1)}), bf16[1,64,1152]{2,1,0:T(8,128)(2,1)}) %reduce-scatter.53.cloned.1.call-update) | async-done | bytes 147472 | tf_op jit(solution)/shard_map/reduce_scatter | solution.py:48
  799.0 7.8 all_gather.71
  827.8 7.2 copy.113
  835.0 7.4 reshape.1841
  856.2 12.6 copy.117
  868.7 4.8 copy.140
  892.8 16.4 copy.88
  909.2 348.2 %scatter_custom_fusion = f32[961,4]{1,0:T(8,128)} fusion(s32[65536]{0:T(1024)} %bitcast.613, f32[65536,4]{1,0:T(8,128)} %copy.88, f32[]{:T(128)} %constant.68.clone.1), kind=kCustom, calls=%fused_computation.465 | custom fusion | flops 262144 | bytes 15888 | tf_op jit(solution)/shard_map/scatter-add | solution.py:145
  1262.0 16.4 copy.90
  1278.4 348.2 %scatter_custom_fusion.1 = f32[961,4]{1,0:T(8,128)} fusion(s32[65536]{0:T(1024)} %bitcast.614, f32[65536,4]{1,0:T(8,128)} %copy.90, f32[]{:T(128)} %constant.68.clone.1), kind=kCustom, calls=%fused_computation.463 | custom fusion | flops 262144 | bytes 15888 | tf_op jit(solution)/shard_map/scatter-add | solution.py:145
  1634.1 16.4 copy.92
  1650.4 347.8 %scatter_fusion = f32[961,4]{1,0:T(8,128)S(1)} fusion(f32[961,4]{1,0:T(8,128)S(1)} %add.668, s32[65536]{0:T(1024)} %bitcast.615, f32[65536,4]{1,0:T(8,128)} %copy.92), kind=kCustom, calls=%fused_computation.4 | custom fusion | flops 262144 | bytes 3407872 | tf_op jit(solution)/shard_map/scatter-add | solution.py:145
  1998.3 22.1 %psum.21 = f32[1,961,4]{2,1,0:T(8,128)} all-reduce(f32[1,961,4]{2,1,0:T(8,128)S(1)} %bitcast.554), channel_id=1, replica_groups=mesh['section'=2,'tensor'=4,'dp'=4] {'dp'}, use_global_device_ids=true, to_apply=%region_77.78 | all-reduce | flops 3844 | bytes 30752 | tf_op jit(solution)/shard_map/psum | solution.py:280
  2025.6 61.5 %all-reduce = (f32[1,2,1152]{2,1,0:T(2,128)}, f32[1,2,1152]{2,1,0:T(2,128)}) all-reduce(f32[1,2,1152]{2,1,0:T(2,128)S(1)} %fusion.414, f32[1,2,1152]{2,1,0:T(2,128)S(1)} %fusion.415), channel_id=1, replica_groups=mesh['section'=2,'tensor'=4,'dp'=4] {'tensor','dp'}, use_global_device_ids=true, to_apply=%region_84.85 | all-reduce | flops 4608 | bytes 36864 | tf_op jit(solution)/shard_map/psum | solution.py:281
  (603 shorter events, 254.2 us)
Async XLA Ops:
  7.2 317.1 %copy-start = (bf16[1,1152,1152]{2,1,0:T(8,128)(2,1)S(1)}, bf16[1,1152,1152]{2,1,0:T(8,128)(2,1)}, u32[]{:S(2)}) copy-start(bf16[1,1152,1152]{2,1,0:T(8,128)(2,1)} %param.20) | copy-start | bytes 7962628
  7.2 305.5 %reduce-scatter.27.cloned.1.call-start = ((), (), s32[]{:S(2)}) async-start(), calls=%async_computation.20 | async-start | bytes 737280 | tf_op jit(solution)/shard_map/reduce_scatter | solution.py:38
  290.2 60.7 %reduce-scatter.29.cloned.1.call-start = ((), (), s32[]{:S(2)}) async-start(), calls=%async_computation.21 | async-start | bytes 737280 | tf_op jit(solution)/shard_map/reduce_scatter | solution.py:38
  324.3 26.7 %copy-start.72 = (bf16[1,64,1152]{2,1,0:T(8,128)(2,1)S(1)}, bf16[1,64,1152]{2,1,0:T(8,128)(2,1)}, u32[]{:S(2)}) copy-start(bf16[1,64,1152]{2,1,0:T(8,128)(2,1)} %reduce-scatter.27.cloned.1.call-done) | copy-start | bytes 442372
  328.9 68.2 %reduce-scatter.31.cloned.1.call-start = ((), (), s32[]{:S(2)}) async-start(), calls=%async_computation.22 | async-start | bytes 737280 | tf_op jit(solution)/shard_map/reduce_scatter | solution.py:38
  352.1 4.8 collective-permute-start
  358.0 65.2 %copy-start.20 = (bf16[1,64,1152]{2,1,0:T(8,128)(2,1)}, bf16[1,64,1152]{2,1,0:T(8,128)(2,1)S(1)}, u32[]{:S(2)}) copy-start(bf16[1,64,1152]{2,1,0:T(8,128)(2,1)S(1)} %get-tuple-element.82) | copy-start | bytes 442372
  374.6 60.8 %reduce-scatter.33.cloned.1.call-start = ((), (), s32[]{:S(2)}) async-start(), calls=%async_computation.23 | async-start | bytes 737280 | tf_op jit(solution)/shard_map/reduce_scatter | solution.py:38
  413.3 77.9 %reduce-scatter.51.cloned.1.call-start = ((), (), s32[]{:S(2)}) async-start(), calls=%async_computation.32 | async-start | bytes 737280 | tf_op jit(solution)/shard_map/reduce_scatter | solution.py:38
  423.4 19.2 copy-start.147
  436.6 4.8 collective-permute-start.1
  437.8 15.0 copy-start.136
  457.7 48.8 %reduce-scatter.35.cloned.1.call-start = ((), (), s32[]{:S(2)}) async-start(), calls=%async_computation.24 | async-start | bytes 737280 | tf_op jit(solution)/shard_map/reduce_scatter | solution.py:38
  484.8 46.4 %reduce-scatter.39.cloned.1.call-start = ((), (), s32[]{:S(2)}) async-start(), calls=%async_computation.26 | async-start | bytes 737280 | tf_op jit(solution)/shard_map/reduce_scatter | solution.py:38
  491.2 79.8 %reduce-scatter.37.cloned.1.call-start = ((), (), s32[]{:S(2)}) async-start(), calls=%async_computation.25 | async-start | bytes 737280 | tf_op jit(solution)/shard_map/reduce_scatter | solution.py:38
  507.7 28.5 %copy-start.131 = (f32[64]{0:T(128)}, f32[64]{0:T(128)S(1)}, u32[]{:S(2)}) copy-start(f32[64]{0:T(128)S(1)} %broadcast_multiply_fusion) | copy-start | bytes 772
  508.8 35.4 %copy-start.146 = (f32[64]{0:T(128)}, f32[64]{0:T(128)S(1)}, u32[]{:S(2)}) copy-start(f32[64]{0:T(128)S(1)} %multiply_reduce_fusion.3) | copy-start | bytes 772
  510.0 34.2 %copy-start.140 = (f32[64]{0:T(128)}, f32[64]{0:T(128)S(1)}, u32[]{:S(2)}) copy-start(f32[64]{0:T(128)S(1)} %fusion.431) | copy-start | bytes 772
  548.8 46.7 %reduce-scatter.41.cloned.1.call-start = ((), (), s32[]{:S(2)}) async-start(), calls=%async_computation.27 | async-start | bytes 737280 | tf_op jit(solution)/shard_map/reduce_scatter | solution.py:48
  563.6 57.0 %reduce-scatter.45.cloned.1.call-start = ((), (), s32[]{:S(2)}) async-start(), calls=%async_computation.29 | async-start | bytes 737280 | tf_op jit(solution)/shard_map/reduce_scatter | solution.py:38
  586.0 75.7 %reduce-scatter.43.cloned.1.call-start = ((), (), s32[]{:S(2)}) async-start(), calls=%async_computation.28 | async-start | bytes 737280 | tf_op jit(solution)/shard_map/reduce_scatter | solution.py:48
  639.6 23.4 %copy-start.148 = (f32[64]{0:T(128)S(1)}, f32[64]{0:T(128)}, u32[]{:S(2)}) copy-start(f32[64]{0:T(128)} %copy-done.147) | copy-start | bytes 772
  639.6 23.4 %copy-start.137 = (f32[64]{0:T(128)S(1)}, f32[64]{0:T(128)}, u32[]{:S(2)}) copy-start(f32[64]{0:T(128)} %copy-done.136) | copy-start | bytes 772
  639.6 67.5 %reduce-scatter.47.cloned.1.call-start = ((), (), s32[]{:S(2)}) async-start(), calls=%async_computation.30 | async-start | bytes 737280 | tf_op jit(solution)/shard_map/reduce_scatter | solution.py:48
  665.8 6.7 collective-permute-start.3
  685.5 62.2 %reduce-scatter.49.cloned.1.call-start = ((), (), s32[]{:S(2)}) async-start(), calls=%async_computation.31 | async-start | bytes 737280 | tf_op jit(solution)/shard_map/reduce_scatter | solution.py:48
  725.5 22.3 %copy-start.130 = (f32[64]{0:T(128)S(1)}, f32[64]{0:T(128)}, u32[]{:S(2)}) copy-start(f32[64]{0:T(128)} %copy-done.129) | copy-start | bytes 772
  725.5 24.6 %copy-start.139 = (f32[64]{0:T(128)S(1)}, f32[64]{0:T(128)}, u32[]{:S(2)}) copy-start(f32[64]{0:T(128)} %copy-done.138) | copy-start | bytes 772
  725.5 69.5 %reduce-scatter.53.cloned.1.call-start = ((), (), s32[]{:S(2)}) async-start(), calls=%async_computation.33 | async-start | bytes 737280 | tf_op jit(solution)/shard_map/reduce_scatter | solution.py:48
  754.0 6.7 collective-permute-start.4
  773.4 1248.9 %reduce-scatter.55.cloned.1.call-start = ((), (), s32[]{:S(2)}) async-start(), calls=%async_computation.34 | async-start | bytes 737280 | tf_op jit(solution)/shard_map/reduce_scatter | solution.py:48
  812.1 1277.8 %reduce-scatter.63.cloned.1.call-start = ((), (), s32[]{:S(2)}) async-start(), calls=%async_computation.38 | async-start | bytes 1105920
  822.4 1270.3 %reduce-scatter.61.cloned.1.call-start = ((), (), s32[]{:S(2)}) async-start(), calls=%async_computation.37 | async-start | bytes 2580480
  842.4 1257.1 %reduce-scatter.57.cloned.1.call-start = ((), (), s32[]{:S(2)}) async-start(), calls=%async_computation.35 | async-start | bytes 3317760 | tf_op jit(solution)/shard_map/reduce_scatter | solution.py:266
  849.2 1252.6 %reduce-scatter.65.cloned.1.call-start = ((), (), s32[]{:S(2)}) async-start(), calls=%async_computation.39 | async-start | bytes 3317760
  873.5 1237.7 %reduce-scatter.59.cloned.1.call-start = ((), (), s32[]{:S(2)}) async-start(), calls=%async_computation.36 | async-start | bytes 3317760 | tf_op jit(solution)/shard_map/reduce_scatter | solution.py:272
  882.4 5.6 collective-permute-start.2
  892.8 365.2 %copy-start.28 = (bf16[4,256,256]{1,2,0:T(8,128)(2,1)S(1)}, bf16[4,256,256]{1,2,0:T(8,128)(2,1)}, u32[]{:S(2)}) copy-start(bf16[4,256,256]{1,2,0:T(8,128)(2,1)} %copy-done.27) | copy-start | bytes 1572868
  1278.4 350.0 %copy-start.124 = (f32[1152]{0:T(1024)S(1)}, f32[1152]{0:T(1024)}, u32[]{:S(2)}) copy-start(f32[1152]{0:T(1024)} %get-tuple-element.48) | copy-start | bytes 13828
  1278.4 350.6 %copy-start.123 = (f32[1152]{0:T(1024)S(1)}, f32[1152]{0:T(1024)}, u32[]{:S(2)}) copy-start(f32[1152]{0:T(1024)} %get-tuple-element.55) | copy-start | bytes 13828
  1998.2 25.2 %copy-start.145 = (f32[64]{0:T(128)S(1)}, f32[64]{0:T(128)}, u32[]{:S(2)}) copy-start(f32[64]{0:T(128)} %copy-done.144) | copy-start | bytes 772
  1998.2 25.3 %copy-start.135 = (f32[64]{0:T(128)S(1)}, f32[64]{0:T(128)}, u32[]{:S(2)}) copy-start(f32[64]{0:T(128)} %copy-done.134) | copy-start | bytes 772
  1998.2 26.6 %copy-start.125 = (f32[1,1,1152]{2,1,0:T(1,128)S(1)}, f32[1,1,1152]{2,1,0:T(1,128)}, u32[]{:S(2)}) copy-start(f32[1,1,1152]{2,1,0:T(1,128)} %stack.130) | copy-start | bytes 13828
  1998.3 26.6 %copy-start.126 = (f32[1,1,1152]{2,1,0:T(1,128)S(1)}, f32[1,1,1152]{2,1,0:T(1,128)}, u32[]{:S(2)}) copy-start(f32[1,1,1152]{2,1,0:T(1,128)} %stack.129) | copy-start | bytes 13828
  1998.3 26.6 %copy-start.127 = (f32[1,1,1152]{2,1,0:T(1,128)S(1)}, f32[1,1,1152]{2,1,0:T(1,128)}, u32[]{:S(2)}) copy-start(f32[1,1,1152]{2,1,0:T(1,128)} %stack.133) | copy-start | bytes 13828
  1998.3 88.8 %copy-start.69 = (bf16[1,64,1152]{2,1,0:T(8,128)(2,1)S(1)}, bf16[1,64,1152]{2,1,0:T(8,128)(2,1)}, u32[]{:S(2)}) copy-start(bf16[1,64,1152]{2,1,0:T(8,128)(2,1)} %copy-done.67) | copy-start | bytes 442372
  2020.4 66.7 %copy-start.42 = (f32[1,64,1152]{2,1,0:T(8,128)S(1)}, f32[1,64,1152]{2,1,0:T(8,128)}, u32[]{:S(2)}) copy-start(f32[1,64,1152]{2,1,0:T(8,128)} %copy-done.41) | copy-start | bytes 884740
  2020.4 66.7 %copy-start.114 = (bf16[1,64,1152]{2,1,0:T(8,128)(2,1)S(1)}, bf16[1,64,1152]{2,1,0:T(8,128)(2,1)}, u32[]{:S(2)}) copy-start(bf16[1,64,1152]{2,1,0:T(8,128)(2,1)} %copy-done.113) | copy-start | bytes 442372
  (134 other events, 477.1 us)
Sparse Core Ops, SparseCore 0:
  290.4 22.2 reduce-scatter.26
  329.0 21.8 reduce-scatter.28
  374.8 22.3 reduce-scatter.30
  413.4 21.9 reduce-scatter.32
  457.8 22.2 reduce-scatter.50
  484.9 21.5 reduce-scatter.34
  509.0 22.0 reduce-scatter.38
  549.0 21.8 reduce-scatter.36
  573.4 22.1 reduce-scatter.40
  598.5 22.0 reduce-scatter.44
  639.7 21.9 reduce-scatter.42
  685.7 21.4 reduce-scatter.46
  725.6 22.0 reduce-scatter.48
  773.5 21.4 reduce-scatter.52
  812.2 21.9 reduce-scatter.54
  837.0 22.1 reduce-scatter.62
  861.3 42.6 reduce-scatter.60
  906.3 53.0 reduce-scatter.56
  961.8 52.3 reduce-scatter.64
  1016.4 52.3 reduce-scatter.58
where the time goes:
time: 2140 us; the launch traced here: 2120 us
  other arithmetic  1120 us (52%)
  local copies, waits for them, and re-layouts  413 us (19%)
  waiting for transfers between devices  242 us (11%)
  blocking collectives  232 us (11%)
  matrix products  87.9 us (4%)
    scatter-add x3, other arithmetic, input_part(): jax.ops.segment_sum(flat_scores, rel_index.reshape(-1), num_segments=(2 *...  1040 us
    gather x2, local copies, waits for them, and re-layouts, per_device(): bias_heads = jnp.transpose(rel_table[0][rel_index], (2, 0, 1))  256 us
    reduce_scatter x9, waiting for transfers between devices, sum_rows(): lax.psum_scatter(terms.astype(jnp.bfloat16), 'tensor', scatter_dimension=...  144 us
    all_gather x12, blocking collectives, gather_rows(): return lax.all_gather(rows, 'tensor', axis=1, tiled=True)  99.8 us
    unnamed x341, local copies, waits for them, and re-layouts  95.7 us
    reduce_scatter x6, waiting for transfers between devices, sum_grads(): lax.psum_scatter(terms.astype(jnp.bfloat16), 'tensor', scatter_dimension=...  78.7 us
    psum x1, blocking collectives, per_device(): lax.psum((small_total[1], small_total[2]), ('tensor', 'dp'))  61.5 us
    transpose x6, local copies, waits for them, and re-layouts, input_part(): jnp.sum(grad_scores.astype(jnp.float32), axis=0).reshape(heads, seq * seq)  53.7 us
  transfers between devices with their start and end apart: 25, of which 18 were waited for; matrix products, arithmetic and copies ran while one was open for 59% of the time, Pallas kernels for 0%

commit v1 on v0

--- a/solution.py
+++ b/solution.py
@@ -48,6 +48,46 @@
     return lax.psum_scatter(
         terms.astype(jnp.bfloat16), "tensor", scatter_dimension=1, tiled=True
     ).astype(jnp.float32)
+
+
+def offset_buckets(rel_index):
+    seq = rel_index.shape[0]
+    grid = int(round(seq**0.5))
+    cells = rel_index.reshape(grid, grid, grid, grid)
+    after = jnp.transpose(cells[0], (1, 0, 2))
+    before = jnp.flip(cells[1:, :, 0, :], axis=0)
+    by_row = jnp.concatenate([before, after], axis=0)
+    right = by_row[:, 0, :]
+    left = jnp.flip(by_row[:, 1:, 0], axis=1)
+    return jnp.concatenate([left, right], axis=1)
+
+
+def expand_bias(table, chosen):
+    heads = table.shape[1]
+    span = int(round(table.shape[0] ** 0.5))
+    grid = (span + 1) // 2
+    by_offset = jnp.dot(chosen, table, precision=lax.Precision.HIGHEST)
+    by_offset = by_offset.T.reshape(heads, span, span)
+    cols = jnp.stack(
+        [by_offset[:, :, grid - 1 - c : span - c] for c in range(grid)], axis=1
+    )
+    bias = jnp.stack([cols[:, :, grid - 1 - r : span - r] for r in range(grid)], axis=1)
+    return bias.reshape(heads, grid * grid, grid * grid)
+
+
+def fold_bias(grads, chosen):
+    heads, seq, _ = grads.shape
+    grid = int(round(seq**0.5))
+    span = 2 * grid - 1
+    cells = grads.reshape(heads, grid, grid, grid, grid)
+    cols = sum(
+        jnp.pad(cells[:, r], ((0, 0), (0, 0), (grid - 1 - r, r), (0, 0))) for r in range(grid)
+    )
+    offsets = sum(
+        jnp.pad(cols[:, c], ((0, 0), (0, 0), (grid - 1 - c, c))) for c in range(grid)
+    )
+    flat = offsets.reshape(heads, span * span)
+    return jnp.einsum("hn,nr->rh", flat, chosen, precision=lax.Precision.HIGHEST)
 
 
 def split_heads(qkv, heads):
@@ -97,7 +137,7 @@
     return (y_mid + mixed, (a_whole, qkv, log_total, attended, y_mid, a_whole2, hidden, active))
 
 
-def input_part(grad_out, x_rows, tvec, cache, weights, bias_heads, rel_index):
+def input_part(grad_out, x_rows, cache, weights, bias_heads):
     w_qkv, w_out, w_fc1, w_fc2, gains, shifts = weights
     a_whole, qkv, log_total, attended, y_mid, a_whole2, hidden, active = cache
     grad_mlp = gather_grads(grad_out.astype(jnp.bfloat16))
@@ -141,10 +181,7 @@
         ],
         axis=2,
     ).astype(jnp.bfloat16)
-    flat_scores = jnp.sum(grad_scores.astype(jnp.float32), axis=0).reshape(heads, seq * seq).T
-    g_table = jax.ops.segment_sum(
-        flat_scores, rel_index.reshape(-1), num_segments=(2 * int(round(seq**0.5)) - 1) ** 2
-    )
+    score_sum = jnp.sum(grad_scores.astype(jnp.float32), axis=0)
     grad_norm1 = sum_grads(
         jnp.einsum("iscj,dcj->isd", grad_qkv, w_qkv, preferred_element_type=jnp.float32)
     )
@@ -152,7 +189,7 @@
     grad_ln1, g_gain1, g_shift1 = norm_back1(grad_norm1)
     grad_x = grad_ymid + grad_ln1
     small_terms = (
-        g_table[None],
+        score_sum,
         jnp.stack([g_gain1, g_gain2])[None],
         jnp.stack([g_shift1, g_shift2])[None],
     )
@@ -165,13 +202,12 @@
         grad_branch,
         a_whole,
         grad_qkv,
-        tvec,
     )
     return (grad_x, small_terms, operands)
 
 
 def weight_part(operands):
-    active, grad_mlp, a_whole2, grad_hidden, attended, grad_branch, a_whole, grad_qkv, tvec = (
+    active, grad_mlp, a_whole2, grad_hidden, attended, grad_branch, a_whole, grad_qkv = (
         operands
     )
     g_fc2 = jnp.einsum("isf,isd->fd", active, grad_mlp, preferred_element_type=jnp.float32)
@@ -179,15 +215,11 @@
     g_out = jnp.einsum("isj,isd->jd", attended, grad_branch, preferred_element_type=jnp.float32)
     g_qkv = jnp.einsum("isd,iscj->dcj", a_whole, grad_qkv, preferred_element_type=jnp.float32)
     token_sums = jnp.sum(grad_qkv.astype(jnp.float32), axis=1)
-    g_time = jnp.einsum(
-        "id,icj->dcj", tvec.astype(jnp.float32), token_sums, precision=lax.Precision.HIGHEST
-    )
-    return (g_qkv[None], g_time[None], g_out[None], g_fc1[None], g_fc2[None])
+    return (g_qkv[None], g_out[None], g_fc1[None], g_fc2[None]), token_sums
 
 
 def settle(operands):
-    weight_terms = weight_part(operands)
-    return tuple(weight_terms)
+    return weight_part(operands)
 
 
 def add_terms(total, terms):
@@ -215,25 +247,25 @@
     per = images.shape[0] // MICRO
     embedded = t_table[timesteps]
     weights = (w_qkv[0], w_out[0], w_fc1[0], w_fc2[0], norm_gain[0], norm_shift[0])
-    bias_heads = jnp.transpose(rel_table[0][rel_index], (2, 0, 1))
+    buckets = offset_buckets(rel_index).reshape(-1, 1)
+    chosen = (buckets == jnp.arange(rel_table.shape[1])[None, :]).astype(jnp.float32)
+    bias_heads = expand_bias(rel_table[0], chosen)
     time_all = jnp.einsum("id,dcj->icj", embedded, w_time[0], preferred_element_type=jnp.float32)
 
     def pick(array, micro):
         return array[micro * per : (micro + 1) * per]
 
     received = jnp.zeros_like(pick(images, 0))
-    inputs, tvecs, times, caches, outputs = ([], [], [], [], [])
+    inputs, times, outputs = ([], [], [])
     for tick in range(MICRO + 1):
         own = min(tick, MICRO - 1)
         before = max(tick - 1, 0)
         block_in = jnp.where(first, pick(images, own), received)
-        tvec = jnp.where(first, pick(embedded, own), pick(embedded, before))
         time_part = jnp.where(first, pick(time_all, own), pick(time_all, before))
         result, cache = forward_block(block_in.astype(jnp.float32), time_part, weights, bias_heads)
         sent = result.astype(jnp.bfloat16)
         received = from_behind(sent, "section", 1)
         inputs.append(block_in)
-        tvecs.append(tvec)
         times.append(time_part)
         if tick >= 1:
             outputs.append(jnp.where(first, received, sent))
@@ -241,6 +273,7 @@
     weight_total = None
     small_total = None
     sent_grads = []
+    tick_sums = []
     for tick in range(MICRO + 1):
         lower = max(tick - 1, 0)
         upper = min(tick + 1, MICRO)
@@ -248,36 +281,35 @@
         grad_in = jnp.where(first, back_in, pick(cotangent, min(tick, MICRO - 1)))
         grad_in = jnp.where(valid, grad_in, jnp.zeros_like(grad_in))
         x_rows = jnp.where(first, inputs[lower], inputs[upper]).astype(jnp.float32)
-        tvec = jnp.where(first, tvecs[lower], tvecs[upper])
         time_part = jnp.where(first, times[lower], times[upper])
         cache = forward_block(x_rows, time_part, weights, bias_heads)[1]
         grad_x, small_terms, operands = input_part(
-            grad_in.astype(jnp.float32), x_rows, tvec, cache, weights, bias_heads, rel_index
+            grad_in.astype(jnp.float32), x_rows, cache, weights, bias_heads
         )
         small_total = add_terms(small_total, small_terms)
         grad_sent = grad_x.astype(jnp.bfloat16)
         back_in = from_behind_2(grad_sent, "section", -1)
-        weight_total = add_terms(weight_total, settle(operands))
+        weight_terms, token_sums = settle(operands)
+        weight_total = add_terms(weight_total, weight_terms)
+        tick_sums.append(token_sums)
         sent_grads.append(grad_sent)
-    weight_total = (
+    g_qkv, g_out, g_fc1, g_fc2 = [
         lax.psum_scatter(
-            weight_total[0].astype(jnp.bfloat16), "dp", scatter_dimension=1, tiled=True
-        ).astype(jnp.float32),
-        lax.psum_scatter(
-            weight_total[1].astype(jnp.bfloat16), "dp", scatter_dimension=1, tiled=True
-        ).astype(jnp.float32),
-        lax.psum_scatter(
-            weight_total[2].astype(jnp.bfloat16), "dp", scatter_dimension=2, tiled=True
-        ).astype(jnp.float32),
-        lax.psum_scatter(
-            weight_total[3].astype(jnp.bfloat16), "dp", scatter_dimension=1, tiled=True
-        ).astype(jnp.float32),
-        lax.psum_scatter(
-            weight_total[4].astype(jnp.bfloat16), "dp", scatter_dimension=2, tiled=True
-        ).astype(jnp.float32),
-    )
-    g_qkv, g_time, g_out, g_fc1, g_fc2 = weight_total
-    g_table = lax.psum(small_total[0], "dp")
+            total.astype(jnp.bfloat16), "dp", scatter_dimension=split, tiled=True
+        ).astype(jnp.float32)
+        for total, split in zip(weight_total, (1, 2, 1, 2))
+    ]
+    image_sums = jnp.concatenate(
+        [jnp.where(first, tick_sums[k + 1], tick_sums[k]) for k in range(MICRO)], axis=0
+    )
+    all_sums = lax.all_gather(image_sums, "dp", axis=0, tiled=True)
+    all_embedded = lax.all_gather(embedded, "dp", axis=0, tiled=True)
+    width = embedded.shape[1] // lax.axis_size("dp")
+    mine = lax.dynamic_slice_in_dim(all_embedded, lax.axis_index("dp") * width, width, axis=1)
+    g_time = jnp.einsum(
+        "id,icj->dcj", mine.astype(jnp.float32), all_sums, precision=lax.Precision.HIGHEST
+    )[None]
+    g_table = lax.psum(fold_bias(small_total[0], chosen), "dp")[None]
     g_gain, g_shift = lax.psum((small_total[1], small_total[2]), ("tensor", "dp"))
     output = jnp.concatenate(outputs, axis=0)
     own_grads = [

time: 2140 us -> 871 us (0.41)
  other arithmetic: 1120 us -> 70.6 us
  local copies, waits for them, and re-layouts: 413 us -> 171 us
    scatter-add x3 -> x0, other arithmetic: 1040 us -> none  [input_part(): jax.ops.segment_sum(flat_scores, rel_index.reshape(-1), num_segments=(2 *...]
    gather x2 -> x0, local copies, waits for them, and re-layouts: 256 us -> none  [per_device(): bias_heads = jnp.transpose(rel_table[0][rel_index], (2, 0, 1))]
    transpose x6 -> x0, local copies, waits for them, and re-layouts: 53.7 us -> none  [input_part(): jnp.sum(grad_scores.astype(jnp.float32), axis=0).reshape(heads, seq * seq)]
    slice x0 -> x4, local copies, waits for them, and re-layouts: none -> 26.6 us  [the longest x1 25.3 us: fold_bias(): cells[:, r]]
    unnamed x341 -> x419, local copies, waits for them, and re-layouts: 95.7 us -> 121 us
    all_gather x0 -> x2, blocking collectives: none -> 24.6 us  [the longest x1 14 us: per_device(): all_sums = lax.all_gather(image_sums, 'dp', axis=0, tiled=True)]
  transfers between devices with their start and end apart: 25 -> 24, of which waited for: 18 -> 19; matrix products, arithmetic and copies ran while one was open for 59% -> 20% of each run, Pallas kernels for 0% -> 0%
where the time goes in v1:
time: 871 us; the launch traced here: 854 us
  blocking collectives  251 us (29%)
  waiting for transfers between devices  249 us (29%)
  local copies, waits for them, and re-layouts  171 us (20%)
  matrix products  87.7 us (10%)
  other arithmetic  70.6 us (8%)
  between operations  16.5 us (2%)
    reduce_scatter x9, waiting for transfers between devices, sum_rows(): lax.psum_scatter(terms.astype(jnp.bfloat16), 'tensor', scatter_dimension=...  153 us
    unnamed x419, local copies, waits for them, and re-layouts  121 us
    all_gather x12, blocking collectives, gather_rows(): return lax.all_gather(rows, 'tensor', axis=1, tiled=True)  100 us
    reduce_scatter x6, waiting for transfers between devices, sum_grads(): lax.psum_scatter(terms.astype(jnp.bfloat16), 'tensor', scatter_dimension=...  78.1 us
    psum x1, blocking collectives, per_device(): lax.psum((small_total[1], small_total[2]), ('tensor', 'dp'))  66.7 us
    all_gather x6, blocking collectives, gather_grads(): return lax.all_gather(rows, 'tensor', axis=1, tiled=True)  47.8 us
    slice x1, local copies, waits for them, and re-layouts, fold_bias(): cells[:, r]  25.3 us
  transfers between devices with their start and end apart: 24, of which 19 were waited for; matrix products, arithmetic and copies ran while one was open for 20% of the time, Pallas kernels for 0%

profile of v1, /device:TPU:9, one launch (start us, length us, event | category | flops | bytes accessed | tf_op | source)
XLA Modules:
  0.0 853.8 jit_solution(11621362174960639202)
XLA Ops:
  18.1 8.1 all_gather.60
  46.1 7.0 reshape.1811
  61.8 22.4 %reduce-scatter.26.cloned.1.call-done = bf16[1,64,1152]{2,1,0:T(8,128)(2,1)} async-done(((bf16[1,256,1152]{2,1,0:T(8,128)(2,1)}), bf16[1,64,1152]{2,1,0:T(8,128)(2,1)}) %reduce-scatter.26.cloned.1.call-update) | async-done | bytes 147472 | tf_op jit(solution)/shard_map/reduce_scatter | solution.py:38
  87.7 8.1 all_gather.61
  95.8 4.6 fusion.79
  100.5 22.0 %reduce-scatter.28.cloned.1.call-done = bf16[1,64,1152]{2,1,0:T(8,128)(2,1)} async-done(((bf16[1,256,1152]{2,1,0:T(8,128)(2,1)}), bf16[1,64,1152]{2,1,0:T(8,128)(2,1)}) %reduce-scatter.28.cloned.1.call-update) | async-done | bytes 147472 | tf_op jit(solution)/shard_map/reduce_scatter | solution.py:38
  130.2 8.3 all_gather.62
  146.5 22.5 %reduce-scatter.30.cloned.1.call-done = bf16[1,64,1152]{2,1,0:T(8,128)(2,1)} async-done(((bf16[1,256,1152]{2,1,0:T(8,128)(2,1)}), bf16[1,64,1152]{2,1,0:T(8,128)(2,1)}) %reduce-scatter.30.cloned.1.call-update) | async-done | bytes 147472 | tf_op jit(solution)/shard_map/reduce_scatter | solution.py:38
  172.5 8.1 all_gather.63
  180.6 4.6 fusion.76
  187.4 8.1 all_gather.66
  195.7 11.6 %reduce-scatter.32.cloned.1.call-done = bf16[1,64,1152]{2,1,0:T(8,128)(2,1)} async-done(((bf16[1,256,1152]{2,1,0:T(8,128)(2,1)}), bf16[1,64,1152]{2,1,0:T(8,128)(2,1)}) %reduce-scatter.32.cloned.1.call-update) | async-done | bytes 147472 | tf_op jit(solution)/shard_map/reduce_scatter | solution.py:38
  216.5 8.5 all_gather.67
  225.1 7.6 all_gather.64
  246.9 9.5 %all_gather.75 = bf16[1,256,1152]{2,1,0:T(8,128)(2,1)} all-gather(bf16[1,64,1152]{2,1,0:T(8,128)(2,1)} %get-tuple-element.139), channel_id=1, replica_groups=mesh['section'=2,'tensor'=4,'dp'=4] {'tensor'}, dimensions={1}, use_global_device_ids=true | all-gather | bytes 737280 | tf_op jit(solution)/shard_map/all_gather | solution.py:34
  264.5 23.3 %reduce-scatter.38.cloned.1.call-done = bf16[1,64,1152]{2,1,0:T(8,128)(2,1)} async-done(((bf16[1,256,1152]{2,1,0:T(8,128)(2,1)}), bf16[1,64,1152]{2,1,0:T(8,128)(2,1)}) %reduce-scatter.38.cloned.1.call-update) | async-done | bytes 147472 | tf_op jit(solution)/shard_map/reduce_scatter | solution.py:38
  291.9 21.1 %reduce-scatter.50.cloned.1.call-done = bf16[1,64,1152]{2,1,0:T(8,128)(2,1)} async-done(((bf16[1,256,1152]{2,1,0:T(8,128)(2,1)}), bf16[1,64,1152]{2,1,0:T(8,128)(2,1)}) %reduce-scatter.50.cloned.1.call-update) | async-done | bytes 147472 | tf_op jit(solution)/shard_map/reduce_scatter | solution.py:38
  317.9 8.1 all_gather.65
  326.0 4.6 fusion.73
  330.7 7.9 all_gather.68
  345.3 7.4 reduce-scatter.36.cloned.1.call-done
  355.8 7.6 all_gather.71
  368.3 9.0 %reduce-scatter.40.cloned.1.call-done = bf16[1,64,1152]{2,1,0:T(8,128)(2,1)} async-done(((bf16[1,256,1152]{2,1,0:T(8,128)(2,1)}), bf16[1,64,1152]{2,1,0:T(8,128)(2,1)}) %reduce-scatter.40.cloned.1.call-update) | async-done | bytes 147472 | tf_op jit(solution)/shard_map/reduce_scatter | solution.py:48
  379.8 22.5 %reduce-scatter.44.cloned.1.call-done = bf16[1,64,1152]{2,1,0:T(8,128)(2,1)} async-done(((bf16[1,256,1152]{2,1,0:T(8,128)(2,1)}), bf16[1,64,1152]{2,1,0:T(8,128)(2,1)}) %reduce-scatter.44.cloned.1.call-update) | async-done | bytes 147472 | tf_op jit(solution)/shard_map/reduce_scatter | solution.py:38
  407.7 7.8 all_gather.69
  421.9 9.2 %all_gather.72 = bf16[1,256,1152]{2,1,0:T(8,128)(2,1)} all-gather(bf16[1,64,1152]{2,1,0:T(8,128)(2,1)} %get-tuple-element.148), channel_id=1, replica_groups=mesh['section'=2,'tensor'=4,'dp'=4] {'tensor'}, dimensions={1}, use_global_device_ids=true | all-gather | bytes 737280 | tf_op jit(solution)/shard_map/all_gather | solution.py:34
  431.1 12.9 %reduce-scatter.42.cloned.1.call-done = bf16[1,64,1152]{2,1,0:T(8,128)(2,1)} async-done(((bf16[1,256,1152]{2,1,0:T(8,128)(2,1)}), bf16[1,64,1152]{2,1,0:T(8,128)(2,1)}) %reduce-scatter.42.cloned.1.call-update) | async-done | bytes 147472 | tf_op jit(solution)/shard_map/reduce_scatter | solution.py:48
  451.6 4.3 collective-permute-done.3
  456.5 8.1 all_gather.70
  468.6 21.6 %reduce-scatter.46.cloned.1.call-done = bf16[1,64,1152]{2,1,0:T(8,128)(2,1)} async-done(((bf16[1,256,1152]{2,1,0:T(8,128)(2,1)}), bf16[1,64,1152]{2,1,0:T(8,128)(2,1)}) %reduce-scatter.46.cloned.1.call-update) | async-done | bytes 147472 | tf_op jit(solution)/shard_map/reduce_scatter | solution.py:48
  495.3 7.6 all_gather.73
  509.4 9.0 %all_gather.76 = bf16[1,256,1152]{2,1,0:T(8,128)(2,1)} all-gather(bf16[1,64,1152]{2,1,0:T(8,128)(2,1)} %get-tuple-element.136), channel_id=1, replica_groups=mesh['section'=2,'tensor'=4,'dp'=4] {'tensor'}, dimensions={1}, use_global_device_ids=true | all-gather | bytes 737280 | tf_op jit(solution)/shard_map/all_gather | solution.py:34
  518.5 13.1 %reduce-scatter.48.cloned.1.call-done = bf16[1,64,1152]{2,1,0:T(8,128)(2,1)} async-done(((bf16[1,256,1152]{2,1,0:T(8,128)(2,1)}), bf16[1,64,1152]{2,1,0:T(8,128)(2,1)}) %reduce-scatter.48.cloned.1.call-update) | async-done | bytes 147472 | tf_op jit(solution)/shard_map/reduce_scatter | solution.py:48
  539.8 4.3 collective-permute-done.4
  544.8 8.0 all_gather.74
  556.8 21.5 %reduce-scatter.52.cloned.1.call-done = bf16[1,64,1152]{2,1,0:T(8,128)(2,1)} async-done(((bf16[1,256,1152]{2,1,0:T(8,128)(2,1)}), bf16[1,64,1152]{2,1,0:T(8,128)(2,1)}) %reduce-scatter.52.cloned.1.call-update) | async-done | bytes 147472 | tf_op jit(solution)/shard_map/reduce_scatter | solution.py:48
  582.3 8.2 all_gather.77
  608.6 5.0 copy.200
  613.6 7.4 reshape.1812
  626.4 9.6 %copy.204 = bf16[1,1152,1152]{1,0,2:T(2,128)(2,1)} copy(bf16[1,1152,1152]{2,1,0:T(8,128)(2,1)S(1)} %fusion.5) | data formatting | bytes 5308416
  636.0 4.5 copy.243
  640.7 10.6 %all-gather.1 = bf16[4,2,1152]{2,1,0:T(2,128)(2,1)S(1)} all-gather(bf16[1,2,1152]{2,1,0:T(2,128)(2,1)S(1)} %bitcast.826), channel_id=2, replica_groups=mesh['section'=2,'tensor'=4,'dp'=4] {'dp'}, dimensions={0}, use_global_device_ids=true | all-gather | bytes 23040 | tf_op jit(solution)/shard_map/all_gather | solution.py:306
  662.8 4.7 add.805
  667.5 25.3 %fusion.498 = (f32[4,1,16,16,16]{2,1,4,3,0:T(1,128)S(1)}, f32[4,1,16,16,16]{2,1,4,3,0:T(1,128)}, f32[4,1,16,16,16]{2,1,4,3,0:T(1,128)}, f32[4,1,16,16,16]{2,1,4,...) fusion(f32[4,16,16,16,16]{2,1,4,3,0:T(8,128)} %add.805), kind=kLoop, calls=%fused_computation.685 | loop fusion | bytes 2097152 | tf_op jit(solution)/shard_map/slice | solution.py:84
  722.8 5.0 pad_add_fusion
  729.0 14.0 %all_gather.79 = f32[8,3,288]{2,1,0:T(4,128)S(1)} all-gather(f32[2,3,288]{2,1,0:T(4,128)S(1)} %pad_maximum_fusion.10), channel_id=1, replica_groups=mesh['section'=2,'tensor'=4,'dp'=4] {'dp'}, dimensions={0}, use_global_device_ids=true | all-gather | bytes 34560 | tf_op jit(solution)/shard_map/all_gather | solution.py:305
  744.5 11.5 %psum.21 = f32[1,961,4]{1,2,0:T(4,128)} all-reduce(f32[1,961,4]{1,2,0:T(4,128)S(1)} %fusion.246), channel_id=1, replica_groups=mesh['section'=2,'tensor'=4,'dp'=4] {'dp'}, use_global_device_ids=true, to_apply=%region_73.74 | all-reduce | flops 3844 | bytes 30752 | tf_op jit(solution)/shard_map/psum | solution.py:312
  761.1 66.7 %all-reduce.32 = (f32[1,2,1152]{2,1,0:T(2,128)}, f32[1,2,1152]{2,1,0:T(2,128)}) all-reduce(f32[1,2,1152]{2,1,0:T(2,128)S(1)} %fusion.450, f32[1,2,1152]{2,1,0:T(2,128)S(1)} %fusion.451), channel_id=1, replica_groups=mesh['section'=2,'tensor'=4,'dp'=4] {'tensor','dp'}, use_global_device_ids=true, to_apply=%region_80.81 | all-reduce | flops 4608 | bytes 36864 | tf_op jit(solution)/shard_map/psum | solution.py:313
  (691 shorter events, 264.7 us)
Async XLA Ops:
  7.2 88.6 %copy-start = (bf16[1,1152,1152]{2,1,0:T(8,128)(2,1)S(1)}, bf16[1,1152,1152]{2,1,0:T(8,128)(2,1)}, u32[]{:S(2)}) copy-start(bf16[1,1152,1152]{2,1,0:T(8,128)(2,1)} %param.20) | copy-start | bytes 7962628
  7.2 77.0 %reduce-scatter.26.cloned.1.call-start = ((), (), s32[]{:S(2)}) async-start(), calls=%async_computation.19 | async-start | bytes 737280 | tf_op jit(solution)/shard_map/reduce_scatter | solution.py:38
  61.7 60.8 %reduce-scatter.28.cloned.1.call-start = ((), (), s32[]{:S(2)}) async-start(), calls=%async_computation.20 | async-start | bytes 737280 | tf_op jit(solution)/shard_map/reduce_scatter | solution.py:38
  95.8 26.7 %copy-start.77 = (bf16[1,64,1152]{2,1,0:T(8,128)(2,1)S(1)}, bf16[1,64,1152]{2,1,0:T(8,128)(2,1)}, u32[]{:S(2)}) copy-start(bf16[1,64,1152]{2,1,0:T(8,128)(2,1)} %reduce-scatter.26.cloned.1.call-done) | copy-start | bytes 442372
  100.4 68.6 %reduce-scatter.30.cloned.1.call-start = ((), (), s32[]{:S(2)}) async-start(), calls=%async_computation.21 | async-start | bytes 737280 | tf_op jit(solution)/shard_map/reduce_scatter | solution.py:38
  123.7 4.8 collective-permute-start
  129.7 65.8 %copy-start.21 = (bf16[1,64,1152]{2,1,0:T(8,128)(2,1)}, bf16[1,64,1152]{2,1,0:T(8,128)(2,1)S(1)}, u32[]{:S(2)}) copy-start(bf16[1,64,1152]{2,1,0:T(8,128)(2,1)S(1)} %get-tuple-element.81) | copy-start | bytes 442372
  146.5 60.8 %reduce-scatter.32.cloned.1.call-start = ((), (), s32[]{:S(2)}) async-start(), calls=%async_computation.22 | async-start | bytes 737280 | tf_op jit(solution)/shard_map/reduce_scatter | solution.py:38
  185.2 78.1 %reduce-scatter.34.cloned.1.call-start = ((), (), s32[]{:S(2)}) async-start(), calls=%async_computation.23 | async-start | bytes 737280 | tf_op jit(solution)/shard_map/reduce_scatter | solution.py:38
  195.7 18.8 %copy-start.164 = (f32[64]{0:T(128)}, f32[64]{0:T(128)S(1)}, u32[]{:S(2)}) copy-start(f32[64]{0:T(128)S(1)} %fusion.402) | copy-start | bytes 772
  208.5 4.8 collective-permute-start.1
  214.5 18.2 %copy-start.25 = (bf16[1,64,1152]{2,1,0:T(8,128)(2,1)}, bf16[1,64,1152]{2,1,0:T(8,128)(2,1)S(1)}, u32[]{:S(2)}) copy-start(bf16[1,64,1152]{2,1,0:T(8,128)(2,1)S(1)} %get-tuple-element.75) | copy-start | bytes 442372
  214.8 17.9 %copy-start.146 = (f32[64]{0:T(128)}, f32[64]{0:T(128)S(1)}, u32[]{:S(2)}) copy-start(f32[64]{0:T(128)S(1)} %fusion.463) | copy-start | bytes 772
  215.2 17.5 %copy-start.16 = (bf16[1,1152,3,288]{1,3,2,0:T(8,128)(2,1)S(1)}, bf16[1,1152,3,288]{1,3,2,0:T(8,128)(2,1)}, u32[]{:S(2)}) copy-start(bf16[1,1152,3,288]{1,3,2,0:T(8,128)(2,1)} %param.17) | copy-start | bytes 5971972
  215.2 17.5 %copy-start.145 = (f32[1,3,288]{2,1,0:T(4,128)S(1)}, f32[1,3,288]{2,1,0:T(4,128)}, u32[]{:S(2)}) copy-start(f32[1,3,288]{2,1,0:T(4,128)} %copy.249) | copy-start | bytes 10372
  240.9 47.0 %reduce-scatter.38.cloned.1.call-start = ((), (), s32[]{:S(2)}) async-start(), calls=%async_computation.25 | async-start | bytes 737280 | tf_op jit(solution)/shard_map/reduce_scatter | solution.py:38
  256.4 56.5 %reduce-scatter.50.cloned.1.call-start = ((), (), s32[]{:S(2)}) async-start(), calls=%async_computation.31 | async-start | bytes 737280 | tf_op jit(solution)/shard_map/reduce_scatter | solution.py:38
  262.6 90.1 %reduce-scatter.36.cloned.1.call-start = ((), (), s32[]{:S(2)}) async-start(), calls=%async_computation.24 | async-start | bytes 737280 | tf_op jit(solution)/shard_map/reduce_scatter | solution.py:38
  288.9 25.1 %copy-start.160 = (f32[64]{0:T(128)}, f32[64]{0:T(128)S(1)}, u32[]{:S(2)}) copy-start(f32[64]{0:T(128)S(1)} %broadcast_multiply_fusion.6) | copy-start | bytes 772
  291.3 21.7 %copy-start.169 = (f32[64]{0:T(128)}, f32[64]{0:T(128)S(1)}, u32[]{:S(2)}) copy-start(f32[64]{0:T(128)S(1)} %multiply_reduce_fusion.5) | copy-start | bytes 772
  291.9 85.5 %copy-start.152 = (f32[64]{0:T(128)}, f32[64]{0:T(128)S(1)}, u32[]{:S(2)}) copy-start(f32[64]{0:T(128)S(1)} %fusion.460) | copy-start | bytes 772
  330.6 46.7 %reduce-scatter.40.cloned.1.call-start = ((), (), s32[]{:S(2)}) async-start(), calls=%async_computation.26 | async-start | bytes 737280 | tf_op jit(solution)/shard_map/reduce_scatter | solution.py:48
  345.3 57.1 %reduce-scatter.44.cloned.1.call-start = ((), (), s32[]{:S(2)}) async-start(), calls=%async_computation.28 | async-start | bytes 737280 | tf_op jit(solution)/shard_map/reduce_scatter | solution.py:38
  368.3 75.7 %reduce-scatter.42.cloned.1.call-start = ((), (), s32[]{:S(2)}) async-start(), calls=%async_computation.27 | async-start | bytes 737280 | tf_op jit(solution)/shard_map/reduce_scatter | solution.py:48
  421.8 23.9 %copy-start.165 = (f32[64]{0:T(128)S(1)}, f32[64]{0:T(128)}, u32[]{:S(2)}) copy-start(f32[64]{0:T(128)} %copy-done.164) | copy-start | bytes 772
  421.8 23.9 %copy-start.149 = (f32[64]{0:T(128)S(1)}, f32[64]{0:T(128)}, u32[]{:S(2)}) copy-start(f32[64]{0:T(128)} %copy-done.148) | copy-start | bytes 772
  421.9 68.3 %reduce-scatter.46.cloned.1.call-start = ((), (), s32[]{:S(2)}) async-start(), calls=%async_computation.29 | async-start | bytes 737280 | tf_op jit(solution)/shard_map/reduce_scatter | solution.py:48
  449.0 6.9 collective-permute-start.3
  466.7 23.5 %copy-start.155 = (f32[64]{0:T(128)S(1)}, f32[64]{0:T(128)}, u32[]{:S(2)}) copy-start(f32[64]{0:T(128)} %copy-done.154) | copy-start | bytes 772
  468.5 63.0 %reduce-scatter.48.cloned.1.call-start = ((), (), s32[]{:S(2)}) async-start(), calls=%async_computation.30 | async-start | bytes 737280 | tf_op jit(solution)/shard_map/reduce_scatter | solution.py:48
  509.4 23.9 %copy-start.167 = (f32[64]{0:T(128)S(1)}, f32[64]{0:T(128)}, u32[]{:S(2)}) copy-start(f32[64]{0:T(128)} %copy-done.166) | copy-start | bytes 772
  509.4 23.9 %copy-start.151 = (f32[64]{0:T(128)S(1)}, f32[64]{0:T(128)}, u32[]{:S(2)}) copy-start(f32[64]{0:T(128)} %copy-done.150) | copy-start | bytes 772
  509.4 69.0 %reduce-scatter.52.cloned.1.call-start = ((), (), s32[]{:S(2)}) async-start(), calls=%async_computation.32 | async-start | bytes 737280 | tf_op jit(solution)/shard_map/reduce_scatter | solution.py:48
  537.2 6.9 collective-permute-start.4
  554.9 23.5 %copy-start.143 = (f32[64]{0:T(128)S(1)}, f32[64]{0:T(128)}, u32[]{:S(2)}) copy-start(f32[64]{0:T(128)} %copy-done.142) | copy-start | bytes 772
  556.7 25.5 %copy-start.74 = (bf16[1,64,1152]{2,1,0:T(8,128)(2,1)S(1)}, bf16[1,64,1152]{2,1,0:T(8,128)(2,1)}, u32[]{:S(2)}) copy-start(bf16[1,64,1152]{2,1,0:T(8,128)(2,1)} %copy-done.73) | copy-start | bytes 442372
  556.7 201.9 %reduce-scatter.54.cloned.1.call-start = ((), (), s32[]{:S(2)}) async-start(), calls=%async_computation.33 | async-start | bytes 737280 | tf_op jit(solution)/shard_map/reduce_scatter | solution.py:48
  596.6 233.1 %reduce-scatter.60.cloned.1.call-start = ((), (), s32[]{:S(2)}) async-start(), calls=%async_computation.36 | async-start | bytes 1105920
  605.3 227.2 %reduce-scatter.58.cloned.1.call-start = ((), (), s32[]{:S(2)}) async-start(), calls=%async_computation.35 | async-start | bytes 2580480
  621.0 216.3 %reduce-scatter.62.cloned.1.call-start = ((), (), s32[]{:S(2)}) async-start(), calls=%async_computation.37 | async-start | bytes 3317760
  640.6 204.2 %reduce-scatter.56.cloned.1.call-start = ((), (), s32[]{:S(2)}) async-start(), calls=%async_computation.34 | async-start | bytes 3317760 | tf_op jit(solution)/shard_map/reduce_scatter | solution.py:297
  651.9 4.5 collective-permute-start.2
  743.0 16.7 %copy-start.147 = (f32[64]{0:T(128)S(1)}, f32[64]{0:T(128)}, u32[]{:S(2)}) copy-start(f32[64]{0:T(128)} %copy-done.146) | copy-start | bytes 772
  744.5 83.3 %copy-start.45 = (f32[1,64,1152]{2,1,0:T(8,128)S(1)}, f32[1,64,1152]{2,1,0:T(8,128)}, u32[]{:S(2)}) copy-start(f32[1,64,1152]{2,1,0:T(8,128)} %copy-done.44) | copy-start | bytes 884740
  744.5 83.3 %copy-start.75 = (bf16[1,64,1152]{2,1,0:T(8,128)(2,1)S(1)}, bf16[1,64,1152]{2,1,0:T(8,128)(2,1)}, u32[]{:S(2)}) copy-start(bf16[1,64,1152]{2,1,0:T(8,128)(2,1)} %copy-done.73) | copy-start | bytes 442372
  744.5 83.4 %copy-start.124 = (bf16[1,64,1152]{2,1,0:T(8,128)(2,1)S(1)}, bf16[1,64,1152]{2,1,0:T(8,128)(2,1)}, u32[]{:S(2)}) copy-start(bf16[1,64,1152]{2,1,0:T(8,128)(2,1)} %copy-done.123) | copy-start | bytes 442372
  744.5 83.4 %copy-start.159 = (f32[64]{0:T(128)S(1)}, f32[64]{0:T(128)}, u32[]{:S(2)}) copy-start(f32[64]{0:T(128)} %copy-done.158) | copy-start | bytes 772
  756.0 73.0 %copy-start.131 = (bf16[1,64,1152]{2,1,0:T(8,128)(2,1)S(1)}, bf16[1,64,1152]{2,1,0:T(8,128)(2,1)}, u32[]{:S(2)}) copy-start(bf16[1,64,1152]{2,1,0:T(8,128)(2,1)} %get-tuple-element.69) | copy-start | bytes 442372
  (152 other events, 550.5 us)
Sparse Core Ops, SparseCore 0:
  61.8 22.3 reduce-scatter.25
  100.5 21.8 reduce-scatter.27
  146.6 22.3 reduce-scatter.29
  185.3 21.9 reduce-scatter.31
  241.0 22.3 reduce-scatter.33
  265.7 22.0 reduce-scatter.37
  290.9 22.0 reduce-scatter.49
  330.8 21.9 reduce-scatter.35
  355.2 22.0 reduce-scatter.39
  380.3 22.0 reduce-scatter.43
  422.0 21.9 reduce-scatter.41
  468.6 21.4 reduce-scatter.45
  509.5 21.9 reduce-scatter.47
  556.9 21.4 reduce-scatter.51
  596.8 21.9 reduce-scatter.53
  620.9 22.3 reduce-scatter.59
  645.5 42.3 reduce-scatter.57
  690.2 53.6 reduce-scatter.61
  746.3 53.6 reduce-scatter.55

commit v2 on v1

v2 whole, which is shorter than its diff:
```python
import functools

import jax
import jax.numpy as jnp
from jax import lax
from jax.experimental import pallas as pl
from jax.experimental.pallas import tpu as pltpu
from jax.sharding import PartitionSpec as P

MESH = pl.DeviceIdType.MESH
F32 = jnp.float32
BF16 = jnp.bfloat16
EPS = 1e-06
GELU_A = 0.7978845608028654
GELU_B = 0.044715
ATT, MLP, DMLP, DATT = range(4)


def mm(a, b):
    return lax.dot_general(a, b, (((1,), (0,)), ((), ())), preferred_element_type=F32)


def mm_nt(a, b):
    return lax.dot_general(a, b, (((1,), (1,)), ((), ())), preferred_element_type=F32)


def mm_tn(a, b):
    return lax.dot_general(a, b, (((0,), (0,)), ((), ())), preferred_element_type=F32)


def head_windows(heads, local):
    width = local // heads
    found = []
    for h in range(heads):
        lo = h * width // 128 * 128
        hi = min(-(-(h + 1) * width // 128) * 128, local)
        found.append((lo, hi, h * width - lo, (h + 1) * width - lo))
    return found


def only(x, start, stop):
    lane = lax.broadcasted_iota(jnp.int32, x.shape, 1)
    return jnp.where((lane >= start) & (lane < stop), x, jnp.zeros_like(x))


def block_kernel(
    cfg,
    x_ref, cot_ref, wq_ref, wo_ref, w1_ref, w2_ref, tp_ref, gain_ref, shift_ref, tx_ref,
    out_ref, ig_ref, gq_ref, go_ref, g1_ref, g2_ref, tok_ref, fold_ref, small_ref,
    xin, gin, mid, gath, keep, rcv_c, rcv_y, snd_c, snd_y, bias, prob, qkv, att, act, dgel,
    xhat, inv, ymid, dy1, dqkv, dh, datt, acc, dsum,
    ag_s, ag_r, rs_s, rs_r, sec_s, sec_r,
):
    count, rows, seq, heads = cfg
    half_rows = 2 * rows
    width = x_ref.shape[-1]
    local = wo_ref.shape[0]
    grid = int(round(seq**0.5))
    windows = head_windows(heads, local)
    scale = (local // heads) ** (-0.5)

    s = lax.axis_index("section")
    t = lax.axis_index("tensor")
    core = t + 1 - 2 * (t % 2)
    far = (t + 2) % 4
    fcore = (core + 2) % 4
    here = t // 2
    there = 1 - here
    own = pl.ds(pl.multiple_of(t * rows, rows), rows)

    barrier = pltpu.get_barrier_semaphore()
    for peer in ({"tensor": core}, {"tensor": far}, {"section": 1 - s}):
        pl.semaphore_signal(barrier, inc=1, device_id=peer, device_id_type=MESH)
    pl.semaphore_wait(barrier, 3)

    def rows_of(owner):
        return pl.ds(pl.multiple_of(owner * rows, rows), rows)

    def half_of(half):
        return pl.ds(pl.multiple_of(half * half_rows, half_rows), half_rows)

    def ag_copy(k, i, which):
        owner, to = ((t, core), (t, far), (far, core))[which]
        ref = gath.at[k, i, rows_of(owner), :]
        return pltpu.make_async_remote_copy(
            src_ref=ref, dst_ref=ref, send_sem=ag_s.at[k, i, which], recv_sem=ag_r.at[k, i, which],
            device_id={"tensor": to}, device_id_type=MESH,
        )

    def ag_start(k, i):
        ag_copy(k, i, 1).start()
        ag_copy(k, i, 0).start()

    def ag_near(k, i):
        ag_copy(k, i, 0).wait_recv()

    def ag_pass(k, i):
        ag_copy(k, i, 1).wait_recv()
        ag_copy(k, i, 2).start()

    def ag_rest(k, i):
        ag_copy(k, i, 2).wait_recv()

    def ag_done(k, i):
        for which in range(3):
            ag_copy(k, i, which).wait_send()

    def rs_copy(k, i, which):
        if which < 2:
            src, dst, to = snd_c.at[k, i, which], rcv_c.at[k, i, which], core
        else:
            src, dst, to = snd_y.at[k, i], rcv_y.at[k, i], far
        return pltpu.make_async_remote_copy(
            src_ref=src, dst_ref=dst, send_sem=rs_s.at[k, i, which], recv_sem=rs_r.at[k, i, which],
            device_id={"tensor": to}, device_id_type=MESH,
        )

    mine = pl.ds(pl.multiple_of((t % 2) * rows, rows), rows)
    other = pl.ds(pl.multiple_of((1 - t % 2) * rows, rows), rows)

    def rs_give(k, i, which, part):
        keep[i, which] = part
        snd_c[k, i, which] = keep[i, which, other, :].astype(BF16)
        rs_copy(k, i, which).start()

    def rs_pass(k, i):
        rs_copy(k, i, 0).wait_recv()
        snd_y[k, i] = (keep[i, 0, mine, :] + rcv_c[k, i, 0].astype(F32)).astype(BF16)
        rs_copy(k, i, 2).start()

    def rs_take(k, i):
        rs_copy(k, i, 1).wait_recv()
        near = keep[i, 1, mine, :] + rcv_c[k, i, 1].astype(F32)
        rs_copy(k, i, 2).wait_recv()
        return near + rcv_y[k, i].astype(F32)

    def rs_done(k, i):
        for which in range(3):
            rs_copy(k, i, which).wait_send()

    def sec_copy(j, src, dst):
        return lambda i: pltpu.make_async_remote_copy(
            src_ref=src.at[i], dst_ref=dst.at[i], send_sem=sec_s.at[j, i], recv_sem=sec_r.at[j, i],
            device_id={"section": 1 - s}, device_id_type=MESH,
        )

    mid_copy = sec_copy(0, mid, xin)
    grad_copy = sec_copy(1, ig_ref, gin)
    out_copy = sec_copy(2, out_ref, out_ref)

    def each_image(body):
        def run(i, carry):
            body(i)
            return carry

        lax.fori_loop(0, count, run, 0)

    def norm(x, which, i):
        mean = jnp.mean(x, axis=-1, keepdims=True)
        centre = x - mean
        root = lax.rsqrt(jnp.mean(centre * centre, axis=-1, keepdims=True) + EPS)
        hat = centre * root
        xhat[which, i] = hat
        inv[which, i] = jnp.broadcast_to(root, (rows, 128))
        return (hat * gain_ref[which : which + 1, :] + shift_ref[which : which + 1, :]).astype(BF16)

    def norm_back(da, which, i):
        hat = xhat[which, i]
        small_ref[which : which + 1, :] += jnp.sum(da * hat, axis=0, keepdims=True)
        small_ref[2 + which : 3 + which, :] += jnp.sum(da, axis=0, keepdims=True)
        dhat = da * gain_ref[which : which + 1, :]
        m1 = jnp.mean(dhat, axis=-1, keepdims=True)
        m2 = jnp.mean(dhat * hat, axis=-1, keepdims=True)
        return inv[which, i][:, :1] * (dhat - m1 - hat * m2)

    small_ref[...] = jnp.zeros_like(small_ref)

    @pl.when(s == 1)
    def _():
        def begin(i):
            gath[DMLP, i, own, :] = cot_ref[i]
            ag_start(DMLP, i)

        each_image(begin)

    def take_input(i):
        @pl.when(s == 0)
        def _():
            xin[i] = x_ref[i]

        @pl.when(s == 1)
        def _():
            mid_copy(i).wait_recv()

        gath[ATT, i, own, :] = norm(xin[i].astype(F32), 0, i)
        ag_start(ATT, i)

    def expand(h, carry):
        for r in range(grid):
            shift = (2 * seq - grid * (grid - 1 - r)) % (2 * seq)
            bias[h, r * grid : (r + 1) * grid, :] = pltpu.roll(tx_ref[h], shift, 1)[:, :seq]
        return carry

    @pl.when(s == 1)
    def _():
        lax.fori_loop(0, heads, expand, 0)
        each_image(lambda i: ag_pass(DMLP, i))

    each_image(take_input)

    @pl.when(s == 0)
    def _():
        lax.fori_loop(0, heads, expand, 0)

    def project(i, half):
        a = gath[ATT, i, half_of(half), :]
        for c in range(3):
            qkv[c, i, half_of(half), :] = (mm_nt(a, wq_ref[c]) + tp_ref[i, c : c + 1, :]).astype(BF16)

    def att_near(i):
        ag_near(ATT, i)
        project(i, here)

    each_image(att_near)

    def att_rest(i):
        ag_pass(ATT, i)
        ag_rest(ATT, i)
        project(i, there)
        acc[...] = jnp.zeros_like(acc)
        for h, (lo, hi, start, stop) in enumerate(windows):
            q = only(qkv[0, i, :, lo:hi], start, stop)
            scores = mm_nt(q, qkv[1, i, :, lo:hi]) * scale + bias[h]
            top = jnp.max(scores, axis=-1, keepdims=True)
            expo = jnp.exp(scores - top)
            p = expo / jnp.sum(expo, axis=-1, keepdims=True)
            prob[i, h] = p
            acc[0, :, lo:hi] += mm(p.astype(BF16), only(qkv[2, i, :, lo:hi], start, stop))
        att[i] = acc[0].astype(BF16)
        rs_give(ATT, i, 0, mm(att[i, half_of(there), :], wo_ref[...]))
        rs_give(ATT, i, 1, mm(att[i, half_of(here), :], wo_ref[...]))
        rs_pass(ATT, i)

    each_image(att_rest)

    def att_end(i):
        y = xin[i].astype(F32) + rs_take(ATT, i)
        ymid[i] = y
        gath[MLP, i, own, :] = norm(y, 1, i)
        ag_start(MLP, i)

    each_image(att_end)

    def mlp_half(i, half, which):
        a = gath[MLP, i, half_of(half), :]
        v = mm(a, w1_ref[...])
        th = jnp.tanh(GELU_A * (v + GELU_B * (v * v * v)))
        up = 0.5 * (1.0 + th)
        act[i, half_of(half), :] = (v * up).astype(BF16)
        dgel[i, half_of(half), :] = up + (0.5 * GELU_A) * v * (1.0 - th * th) * (
            1.0 + (3.0 * GELU_B) * (v * v)
        )
        rs_give(MLP, i, which, mm(act[i, half_of(half), :], w2_ref[...]))

    def mlp_near(i):
        ag_near(MLP, i)
        mlp_half(i, here, 1)

    each_image(mlp_near)

    def mlp_rest(i):
        ag_pass(MLP, i)
        ag_rest(MLP, i)
        mlp_half(i, there, 0)
        rs_pass(MLP, i)

    each_image(mlp_rest)

    def mlp_end(i):
        mid[i] = (ymid[i] + rs_take(MLP, i)).astype(BF16)

        @pl.when(s == 0)
        def _():
            mid_copy(i).start()

        @pl.when(s == 1)
        def _():
            out_ref[i] = mid[i]
            out_copy(i).start()

    each_image(mlp_end)

    def take_grad(i):
        mid_copy(i).wait_send()
        grad_copy(i).wait_recv()
        gath[DMLP, i, own, :] = gin[i]
        ag_start(DMLP, i)

    @pl.when(s == 0)
    def _():
        each_image(take_grad)

    @pl.when(s == 1)
    def _():
        def keep_cot(i):
            gin[i] = cot_ref[i]

        each_image(keep_cot)

    def dmlp_half(i, half, which):
        dact = mm_nt(gath[DMLP, i, half_of(half), :], w2_ref[...])
        dh[i, half_of(half), :] = (dact * dgel[i, half_of(half), :]).astype(BF16)
        rs_give(DMLP, i, which, mm_nt(dh[i, half_of(half), :], w1_ref[...]))

    def dmlp_near(i):
        ag_near(DMLP, i)
        dmlp_half(i, here, 1)

    each_image(dmlp_near)

    def dmlp_rest(i):
        @pl.when(s == 0)
        def _():
            ag_pass(DMLP, i)

        ag_rest(DMLP, i)
        dmlp_half(i, there, 0)
        rs_pass(DMLP, i)

    each_image(dmlp_rest)

    tokens = count * seq

    def weight_grad(k, right, dst):
        left = gath[k].reshape(tokens, width)
        dst[...] = mm_tn(left, right.reshape(tokens, right.shape[-1])).astype(BF16)

    weight_grad(MLP, dh[...], g1_ref)

    def dmlp_end(i):
        grad = gin[i].astype(F32) + norm_back(rs_take(DMLP, i), 1, i)
        dy1[i] = grad
        gath[DATT, i, own, :] = grad.astype(BF16)
        ag_start(DATT, i)

    each_image(dmlp_end)

    weight_grad(DMLP, act[...], g2_ref)

    def datt_part(i, half):
        datt[i, half_of(half), :] = mm_nt(gath[DATT, i, half_of(half), :], wo_ref[...]).astype(BF16)

    def datt_near(i):
        ag_near(DATT, i)
        datt_part(i, here)

    each_image(datt_near)

    def datt_rest(i):
        ag_pass(DATT, i)
        ag_rest(DATT, i)
        datt_part(i, there)
        acc[...] = jnp.zeros_like(acc)
        for h, (lo, hi, start, stop) in enumerate(windows):
            q = only(qkv[0, i, :, lo:hi], start, stop)
            k = only(qkv[1, i, :, lo:hi], start, stop)
            d = only(datt[i, :, lo:hi], start, stop)
            p = prob[i, h]
            dp = mm_nt(d, qkv[2, i, :, lo:hi])
            inner = jnp.sum(p * dp, axis=-1, keepdims=True)
            ds = (p * (dp - inner)).astype(BF16)

            @pl.when(i == 0)
            def _():
                dsum[h] = ds.astype(F32)

            @pl.when(i > 0)
            def _():
                dsum[h] += ds.astype(F32)

            acc[0, :, lo:hi] += mm(ds, k)
            acc[1, :, lo:hi] += mm_tn(ds, q)
            acc[2, :, lo:hi] += mm_tn(p.astype(BF16), d)
        for c, by in enumerate((scale, scale, 1.0)):
            part = (acc[c] * by).astype(BF16)
            dqkv[c, i] = part
            tok_ref[i, c : c + 1, :] = jnp.sum(part.astype(F32), axis=0, keepdims=True)
        for which, half in ((0, there), (1, here)):
            rs_give(
                DATT, i, which,
                sum(mm(dqkv[c, i, half_of(half), :], wq_ref[c]) for c in range(3)),
            )
        rs_pass(DATT, i)

    each_image(datt_rest)

    left = gath[ATT].reshape(tokens, width)
    for c in range(3):
        gq_ref[c] = mm_tn(left, dqkv[c].reshape(tokens, local)).astype(BF16)

    def datt_end(i):
        grad = dy1[i] + norm_back(rs_take(DATT, i), 0, i)
        ig_ref[i] = grad.astype(BF16)

        @pl.when(s == 1)
        def _():
            grad_copy(i).start()

    each_image(datt_end)

    weight_grad(DATT, att[...], go_ref)

    def fold(h, carry):
        total = jnp.zeros((grid, 2 * seq), F32)
        for r in range(grid):
            part = dsum[h, r * grid : (r + 1) * grid, :]
            wide = jnp.concatenate([part, jnp.zeros_like(part)], axis=1)
            shift = grid * (grid - 1 - r)
            total += wide if shift == 0 else pltpu.roll(wide, shift, 1)
        fold_ref[h] = total
        return carry

    lax.fori_loop(0, heads, fold, 0)

    def finish(i):
        for k in range(4):
            ag_done(k, i)
            rs_done(k, i)

        @pl.when(s == 0)
        def _():
            out_copy(i).wait_recv()

        @pl.when(s == 1)
        def _():
            out_copy(i).wait_send()
            grad_copy(i).wait_send()

    each_image(finish)


def run_block(x, cot, wq, wo, w1, w2, tp, gain, shift, tx, seq):
    count, rows, width = x.shape
    heads = tx.shape[0]
    local = wo.shape[0]
    hidden = w1.shape[1]
    dims = (count, rows, seq, heads)
    out_shape = [
        jax.ShapeDtypeStruct((count, rows, width), BF16),
        jax.ShapeDtypeStruct((count, rows, width), BF16),
        jax.ShapeDtypeStruct((3, width, local), BF16),
        jax.ShapeDtypeStruct((width, local), BF16),
        jax.ShapeDtypeStruct((width, hidden), BF16),
        jax.ShapeDtypeStruct((width, hidden), BF16),
        jax.ShapeDtypeStruct((count, 3, local), F32),
        jax.ShapeDtypeStruct(tx.shape, F32),
        jax.ShapeDtypeStruct((4, width), F32),
    ]
    vm = pltpu.VMEM
    dma = pltpu.SemaphoreType.DMA
    scratch = [
        vm((count, rows, width), BF16),
        vm((count, rows, width), BF16),
        vm((count, rows, width), BF16),
        vm((4, count, seq, width), BF16),
        vm((count, 2, 2 * rows, width), F32),
        vm((4, count, 2, rows, width), BF16),
        vm((4, count, rows, width), BF16),
        vm((4, count, 2, rows, width), BF16),
        vm((4, count, rows, width), BF16),
        vm((heads, seq, seq), F32),
        vm((count, heads, seq, seq), F32),
        vm((3, count, seq, local), BF16),
        vm((count, seq, local), BF16),
        vm((count, seq, hidden), BF16),
        vm((count, seq, hidden), F32),
        vm((2, count, rows, width), F32),
        vm((2, count, rows, 128), F32),
        vm((count, rows, width), F32),
        vm((count, rows, width), F32),
        vm((3, count, seq, local), BF16),
        vm((count, seq, hidden), BF16),
        vm((count, seq, local), BF16),
        vm((3, seq, local), F32),
        vm((heads, seq, seq), F32),
        dma((4, count, 3)),
        dma((4, count, 3)),
        dma((4, count, 3)),
        dma((4, count, 3)),
        dma((3, count)),
        dma((3, count)),
    ]
    whole = pl.BlockSpec(memory_space=pltpu.VMEM)
    return pl.pallas_call(
        functools.partial(block_kernel, dims),
        out_shape=out_shape,
        in_specs=[whole] * 10,
        out_specs=[whole] * len(out_shape),
        scratch_shapes=scratch,
        compiler_params=pltpu.CompilerParams(
            collective_id=0, has_side_effects=True, vmem_limit_bytes=62 * 2**20
        ),
        name="blocks",
    )(x, cot, wq, wo, w1, w2, tp, gain, shift, tx)


def offset_buckets(rel_index):
    seq = rel_index.shape[0]
    grid = int(round(seq**0.5))
    cells = rel_index.reshape(grid, grid, grid, grid)
    after = jnp.transpose(cells[0], (1, 0, 2))
    before = jnp.flip(cells[1:, :, 0, :], axis=0)
    by_row = jnp.concatenate([before, after], axis=0)
    right = by_row[:, 0, :]
    left = jnp.flip(by_row[:, 1:, 0], axis=1)
    return jnp.concatenate([left, right], axis=1)


def spread_table(table, chosen):
    heads, buckets = table.shape
    span = int(round(buckets**0.5))
    grid = (span + 1) // 2
    by_offset = jnp.dot(table, chosen.T, precision=lax.Precision.HIGHEST).reshape(heads, span, span)
    cols = jnp.stack([by_offset[:, :, grid - 1 - c : span - c] for c in range(grid)], axis=1)
    cols = jnp.pad(cols, ((0, 0), (0, 0), (0, 1), (0, 0)))
    return cols.reshape(heads, grid, (span + 1) * grid)


def gather_table(folded, chosen):
    heads, grid, _ = folded.shape
    span = 2 * grid - 1
    cols = folded.reshape(heads, grid, span + 1, grid)[:, :, :span]
    offsets = sum(jnp.pad(cols[:, c], ((0, 0), (0, 0), (grid - 1 - c, c))) for c in range(grid))
    flat = offsets.reshape(heads, span * span)
    return jnp.dot(chosen.T, flat.T, precision=lax.Precision.HIGHEST)


def per_device(
    images, timesteps, t_table, rel_index, w_qkv, w_time, w_out, w_fc1, w_fc2, rel_table,
    norm_gain, norm_shift, cotangent,
):
    seq = rel_index.shape[0]
    buckets = offset_buckets(rel_index).reshape(-1, 1)
    chosen = (buckets == jnp.arange(rel_table.shape[1])[None, :]).astype(F32)
    tx = spread_table(rel_table[0].T, chosen)
    embedded = t_table[timesteps]
    wq = jnp.transpose(w_qkv[0], (1, 2, 0))
    wt = jnp.transpose(w_time[0], (1, 2, 0))
    tp = jnp.einsum("id,cjd->icj", embedded, wt, preferred_element_type=F32)
    output, in_grad, gq, go, g1, g2, tok, folded, small = run_block(
        images, cotangent, wq, w_out[0], w_fc1[0], w_fc2[0], tp, norm_gain[0], norm_shift[0], tx, seq
    )

    def scatter(grad, axis):
        return lax.psum_scatter(grad, "dp", scatter_dimension=axis, tiled=True).astype(F32)

    g_qkv = jnp.transpose(scatter(gq, 1), (1, 0, 2))[None]
    g_fc1 = scatter(g1, 0)[None]
    g_fc2 = scatter(g2, 0).T[None]
    g_out = scatter(go, 0).T[None]
    all_sums = lax.all_gather(tok, "dp", axis=0, tiled=True)
    all_embedded = lax.all_gather(embedded, "dp", axis=0, tiled=True)
    cut = embedded.shape[1] // lax.axis_size("dp")
    mine = lax.dynamic_slice_in_dim(all_embedded, lax.axis_index("dp") * cut, cut, axis=1)
    g_time = jnp.einsum(
        "id,icj->dcj", mine.astype(F32), all_sums, precision=lax.Precision.HIGHEST
    )[None]
    g_table = lax.psum(gather_table(folded, chosen), "dp")[None]
    small = lax.psum(small, ("tensor", "dp"))
    return (
        output, in_grad[None], g_qkv, g_time, g_out, g_fc1, g_fc2, g_table,
        small[None, :2], small[None, 2:],
    )


def solution(mesh):
    in_specs = (
        P("dp", "tensor", None),
        P("dp"),
        P(),
        P(),
        P("section", None, None, "tensor"),
        P("section", None, None, "tensor"),
        P("section", "tensor", None),
        P("section", None, "tensor"),
        P("section", "tensor", None),
        P("section", None, "tensor"),
        P("section", None, None),
        P("section", None, None),
        P("dp", "tensor", None),
    )
    out_specs = (
        P("dp", "tensor", None),
        P("section", "dp", "tensor", None),
        P("section", "dp", None, "tensor"),
        P("section", "dp", None, "tensor"),
        P("section", "tensor", "dp"),
        P("section", "dp", "tensor"),
        P("section", "tensor", "dp"),
        P("section", None, "tensor"),
        P("section", None, None),
        P("section", None, None),
    )
    return jax.shard_map(
        per_device, mesh=mesh, in_specs=in_specs, out_specs=out_specs, check_vma=False
    )
```

time: 871 us -> 385 us (0.44); the launches traced: 854 us -> 382 us
  waiting for transfers between devices: 249 us -> 77.6 us
  Pallas kernels: 0 us -> 161 us
  local copies, waits for them, and re-layouts: 171 us -> 14.6 us
  blocking collectives: 251 us -> 100 us
  matrix products: 87.7 us -> 5.88 us
  other arithmetic: 70.6 us -> 8.13 us
    pallas_call x0 -> x1, Pallas kernels: none -> 161 us  [run_block(): pl.pallas_call(functools.partial(block_kernel, dims), out_shape=out_shape...]
    reduce_scatter x16 -> x4, waiting for transfers between devices: 231 us -> 75.7 us  [scatter(): lax.psum_scatter(grad, 'dp', scatter_dimension=axis, tiled=True).astype(F32)]
    all_gather x19 -> x1, blocking collectives: 162 us -> 12.3 us  [per_device(): all_sums = lax.all_gather(tok, 'dp', axis=0, tiled=True)]
    unnamed x419 -> x37, local copies, waits for them, and re-layouts: 121 us -> 4.09 us
    dot_general x70 -> x4, matrix products: 87.7 us -> 5.88 us  [the longest x1 1.87 us: spread_table(): jnp.dot(table, chosen.T, precision=lax.Precision.HIGHEST)]
    reduce_sum x42 -> x0, other arithmetic: 39.3 us -> none  [the longest x15 16.4 us: layer_norm(): centre = rows - jnp.mean(rows, axis=-1, keepdims=True)]
    slice x8 -> x0, local copies, waits for them, and re-layouts: 27.5 us -> none  [the longest x1 25.3 us: fold_bias(): cells[:, r]]
    ppermute x5 -> x0, waiting for transfers between devices: 17.7 us -> none  [the longest x3 9.19 us: from_behind(): lax.ppermute(x, axis, [(i, (i + by) % length) for i in range(length)])]
  transfers between devices with their start and end apart: 24 -> 4, of which waited for: 19 -> 2; matrix products, arithmetic and copies ran while one was open for 20% -> 3% of each run, Pallas kernels for 0% -> 0%
where the time goes in v2:
time: 385 us; the launch traced here: 382 us
  Pallas kernels  161 us (42%)
  blocking collectives  100 us (26%)
  waiting for transfers between devices  77.6 us (20%)
  local copies, waits for them, and re-layouts  14.6 us (4%)
  between operations  14 us (4%)
  other arithmetic  8.13 us (2%)
  matrix products  5.88 us (2%)
    pallas_call x1, Pallas kernels, run_block(): pl.pallas_call(functools.partial(block_kernel, dims), out_shape=out_shape...  161 us
    reduce_scatter x4, waiting for transfers between devices, scatter(): lax.psum_scatter(grad, 'dp', scatter_dimension=axis, tiled=True).astype(F32)  75.7 us
    psum x1, blocking collectives, per_device(): small = lax.psum(small, ('tensor', 'dp'))  61.1 us
    psum x1, blocking collectives, per_device(): g_table = lax.psum(gather_table(folded, chosen), 'dp')[None]  15.7 us
    all_gather x1, blocking collectives, per_device(): all_sums = lax.all_gather(tok, 'dp', axis=0, tiled=True)  12.3 us
    all_gather x1, blocking collectives, per_device(): all_embedded = lax.all_gather(embedded, 'dp', axis=0, tiled=True)  11.2 us
  transfers between devices with their start and end apart: 4, of which 2 were waited for; matrix products, arithmetic and copies ran while one was open for 3% of the time, Pallas kernels for 0%

profile of v2, /device:TPU:9, one launch (start us, length us, event | category | flops | bytes accessed | tf_op | source)
XLA Modules:
  0.0 382.0 jit_solution(14610354250126407981)
XLA Ops:
  7.3 3.0 reshape.39
  10.3 0.1 squeeze.92
  10.4 1.3 slice.172
  11.8 2.5 gather_fusion
  14.4 0.7 fusion.2
  15.1 0.6 copy.82.tp_ref
  15.7 0.3 copy.102
  16.1 0.1 eq.15
  16.3 1.9 fusion.6
  18.1 0.2 reshape.40
  18.5 0.1 fusion.22
  18.5 0.1 fusion.21
  18.6 0.1 fusion.20
  18.7 0.1 fusion.19
  19.0 0.1 fusion.16
  19.1 0.1 fusion.15
  19.2 0.1 fusion.14
  19.2 0.1 fusion.13
  19.3 0.1 fusion.12
  19.4 0.1 fusion.11
  19.5 0.1 fusion.10
  19.6 0.1 pad.68
  19.8 0.6 reshape.62
  20.3 0.7 copy.100.tx_ref
  21.0 161.4 %blocks.1 = (bf16[2,64,1152]{2,1,0:T(8,128)(2,1)}, bf16[2,64,1152]{2,1,0:T(8,128)(2,1)}, bf16[3,1152,288]{2,1,0:T(8,128)(2,1)}, bf16[1152,288]{1,0:T(8,128)(2,1)...) custom-call(bf16[2,64,1152]{2,1,0:T(8,128)(2,1)} %x_ref.1, ...), custom_call_target="tpu_custom_call" | custom-call | tf_op jit(solution)/shard_map/blocks/pallas_call | solution.py:494
  182.5 0.7 reduce-scatter.5.cloned.1.call-update
  183.3 0.7 reduce-scatter.9.cloned.1.call-update
  184.0 0.5 reduce-scatter.11.cloned.1.call-update
  184.5 11.2 %all-gather.1 = bf16[4,2,1152]{2,1,0:T(2,128)(2,1)S(1)} all-gather(bf16[1,2,1152]{2,1,0:T(2,128)(2,1)S(1)} %bitcast.196), channel_id=2, replica_groups=mesh['section'=2,'tensor'=4,'dp'=4] {'dp'}, dimensions={0}, use_global_device_ids=true | all-gather | bytes 23040 | tf_op jit(solution)/shard_map/all_gather | solution.py:562
  195.8 0.4 reshape.42
  196.1 0.1 slice_bitcast_fusion.15
  196.2 0.3 pad_add_fusion
  196.6 0.1 reshape.43
  196.7 61.1 %psum.15 = f32[4,1152]{1,0:T(4,128)S(1)} all-reduce(f32[4,1152]{1,0:T(4,128)S(1)} %copy-done.4), channel_id=1, replica_groups=mesh['section'=2,'tensor'=4,'dp'=4] {'tensor','dp'}, use_global_device_ids=true, to_apply=%region_5.6 | all-reduce | flops 4608 | bytes 36864 | tf_op jit(solution)/shard_map/psum | solution.py:569
  257.7 12.3 %all_gather.7 = f32[8,3,288]{2,1,0:T(4,128)S(1)} all-gather(f32[2,3,288]{2,1,0:T(4,128)S(1)} %copy-done.5), channel_id=1, replica_groups=mesh['section'=2,'tensor'=4,'dp'=4] {'dp'}, dimensions={0}, use_global_device_ids=true | all-gather | bytes 34560 | tf_op jit(solution)/shard_map/all_gather | solution.py:561
  270.0 1.5 fusion.7
  271.5 15.7 %psum.14 = f32[1,961,4]{1,2,0:T(4,128)} all-reduce(f32[1,961,4]{1,2,0:T(4,128)S(1)} %fusion.7), channel_id=1, replica_groups=mesh['section'=2,'tensor'=4,'dp'=4] {'dp'}, use_global_device_ids=true, to_apply=%region_4.5 | all-reduce | flops 3844 | bytes 30752 | tf_op jit(solution)/shard_map/psum | solution.py:568
  287.2 1.9 convolution_bitcast_fusion
  289.1 0.6 slice_bitcast_fusion.32
  289.7 1.0 convert_bitcast_fusion.2
  290.6 1.0 copy.99
  291.6 2.2 convert_bitcast_fusion.1
  293.9 24.1 %reduce-scatter.9.cloned.1.call-done = bf16[288,1152]{1,0:T(8,128)(2,1)} async-done(((bf16[1152,1152]{1,0:T(8,128)(2,1)}), bf16[288,1152]{1,0:T(8,128)(2,1)}) %reduce-scatter.9.cloned.1.call-update) | async-done | bytes 663568 | tf_op jit(solution)/shard_map/reduce_scatter | solution.py:555
  318.0 2.2 bitcast_convert_fusion
  320.2 51.6 %reduce-scatter.11.cloned.1.call-done = bf16[288,1152]{1,0:T(8,128)(2,1)} async-done(((bf16[1152,1152]{1,0:T(8,128)(2,1)}), bf16[288,1152]{1,0:T(8,128)(2,1)}) %reduce-scatter.11.cloned.1.call-update) | async-done | bytes 663568 | tf_op jit(solution)/shard_map/reduce_scatter | solution.py:555
  371.8 2.2 convert_bitcast_fusion
  374.1 0.7 copy.139
  374.8 0.7 copy.140
  (39 shorter events, 0.9 us)
Async XLA Ops:
  7.2 7.2 %copy-start = (bf16[1,1152,3,288]{1,3,2,0:T(8,128)(2,1)S(1)}, bf16[1,1152,3,288]{1,3,2,0:T(8,128)(2,1)}, u32[]{:S(2)}) copy-start(bf16[1,1152,3,288]{1,3,2,0:T(8,128)(2,1)} %param.18) | copy-start | bytes 5971972
  7.2 3.1 slice-start
  7.2 282.5 %reduce-scatter.7.cloned.1.call-start = ((), (), s32[]{:S(2)}) async-start(), calls=%async_computation.5 | async-start | bytes 1105920 | tf_op jit(solution)/shard_map/reduce_scatter | solution.py:555
  7.2 4.6 %copy-start.7 = (s32[2]{0:T(128)S(1)}, s32[2]{0:T(128)}, u32[]{:S(2)}) copy-start(s32[2]{0:T(128)} %param.14) | copy-start | bytes 28
  10.4 5.9 %copy-start.6 = (f32[1,961,4]{1,2,0:T(4,128)S(1)}, f32[1,961,4]{1,2,0:T(4,128)}, u32[]{:S(2)}) copy-start(f32[1,961,4]{1,2,0:T(4,128)} %param.22) | copy-start | bytes 46132
  182.5 109.2 %reduce-scatter.5.cloned.1.call-start = ((), (), s32[]{:S(2)}) async-start(), calls=%async_computation.4 | async-start | bytes 3317760 | tf_op jit(solution)/shard_map/reduce_scatter | solution.py:555
  183.2 134.8 %reduce-scatter.9.cloned.1.call-start = ((), (), s32[]{:S(2)}) async-start(), calls=%async_computation.6 | async-start | bytes 3317760 | tf_op jit(solution)/shard_map/reduce_scatter | solution.py:555
  183.9 11.8 %copy-start.3 = (f32[4,16,512]{2,1,0:T(8,128)S(1)}, f32[4,16,512]{2,1,0:T(8,128)}, u32[]{:S(2)}) copy-start(f32[4,16,512]{2,1,0:T(8,128)} %get-tuple-element.26) | copy-start | bytes 393220
  184.0 187.9 %reduce-scatter.11.cloned.1.call-start = ((), (), s32[]{:S(2)}) async-start(), calls=%async_computation.7 | async-start | bytes 3317760 | tf_op jit(solution)/shard_map/reduce_scatter | solution.py:555
  195.7 0.9 copy-start.4
  195.8 62.0 %copy-start.5 = (f32[2,3,288]{2,1,0:T(4,128)S(1)}, f32[2,3,288]{2,1,0:T(4,128)}, u32[]{:S(2)}) copy-start(f32[2,3,288]{2,1,0:T(4,128)} %get-tuple-element.22) | copy-start | bytes 20740
  293.9 80.2 %copy-start.2 = (bf16[2,64,1152]{2,1,0:T(8,128)(2,1)S(1)}, bf16[2,64,1152]{2,1,0:T(8,128)(2,1)}, u32[]{:S(2)}) copy-start(bf16[2,64,1152]{2,1,0:T(8,128)(2,1)} %get-tuple-element.86) | copy-start | bytes 884740
  293.9 80.9 %copy-start.1 = (bf16[2,64,1152]{2,1,0:T(8,128)(2,1)S(1)}, bf16[2,64,1152]{2,1,0:T(8,128)(2,1)}, u32[]{:S(2)}) copy-start(bf16[2,64,1152]{2,1,0:T(8,128)(2,1)} %get-tuple-element.20) | copy-start | bytes 884740
Sparse Core Ops, SparseCore 0:
  182.6 23.1 reduce-scatter.6
  208.1 55.3 reduce-scatter.4
  265.8 52.1 reduce-scatter.8
  320.2 51.6 reduce-scatter.10

commit v3 on v2

v3 whole, which is shorter than its diff:
```python
import functools

import jax
import jax.numpy as jnp
from jax import lax
from jax.experimental import pallas as pl
from jax.experimental.pallas import tpu as pltpu
from jax.sharding import PartitionSpec as P

MESH = pl.DeviceIdType.MESH
F32 = jnp.float32
BF16 = jnp.bfloat16
EPS = 1e-06
GELU_A = 0.7978845608028654
GELU_B = 0.044715
ATT, MLP, DMLP, DATT = range(4)


def mm(a, b):
    return lax.dot_general(a, b, (((1,), (0,)), ((), ())), preferred_element_type=F32)


def mm_nt(a, b):
    return lax.dot_general(a, b, (((1,), (1,)), ((), ())), preferred_element_type=F32)


def mm_tn(a, b):
    return lax.dot_general(a, b, (((0,), (0,)), ((), ())), preferred_element_type=F32)


def head_windows(heads, local):
    width = local // heads
    found = []
    for h in range(heads):
        lo = h * width // 128 * 128
        hi = min(-(-(h + 1) * width // 128) * 128, local)
        found.append((lo, hi, h * width - lo, (h + 1) * width - lo))
    return found


def only(x, start, stop):
    lane = lax.broadcasted_iota(jnp.int32, x.shape, 1)
    return jnp.where((lane >= start) & (lane < stop), x, jnp.zeros_like(x))


def in_thirds(x):
    high = x.astype(BF16)
    rest = x - high.astype(F32)
    middle = rest.astype(BF16)
    low = (rest - middle.astype(F32)).astype(BF16)
    return jnp.concatenate([high, middle, low], axis=0)


def add_thirds(x):
    rows = x.shape[0] // 3
    return x[:rows] + x[rows : 2 * rows] + x[2 * rows :]


def wider(x, lanes):
    return jnp.concatenate([x, jnp.zeros((x.shape[0], lanes - x.shape[1]), x.dtype)], axis=1)


def block_kernel(
    cfg,
    x_ref, cot_ref, wq_hbm, wt_hbm, wo_hbm, w1_hbm, w2_hbm, temb_ref, gain_ref, shift_ref, rel_ref, tab_ref,
    out_ref, ig_ref, tot_ref, tok_ref, emb_ref, gtab_ref, small_ref,
    wq_ref, wt_ref, wo_ref, w1_ref, w2_ref, tp_ref, tx_ref, chosen, tab, partial, arrived,
    tiny_s, small_r,
    xin, gin, mid, gath, keep, rcv_c, rcv_y, snd_c, snd_y, bias, prob, qkv, att, act, dgel,
    xhat, inv, ymid, dy1, dqkv, dh, datt, acc, turned, far_att,
    load_s, ag_s, ag_r, rs_s, rs_r, sec_s, sec_r, ch_s, ch_r, ti_s, ti_r, sm_s, sm_r,
):
    count, rows, seq, heads, ring, chained = cfg
    half_rows = 2 * rows
    width = x_ref.shape[-1]
    local = wo_ref.shape[0]
    grid = int(round(seq**0.5))
    windows = head_windows(heads, local)
    scale = (local // heads) ** (-0.5)
    blocks = partial.shape[1] if chained else tot_ref.shape[1]
    cut = width // blocks
    lanes = dqkv.shape[-1]
    parts = partial if chained else tot_ref

    s = lax.axis_index("section")
    t = lax.axis_index("tensor")
    z = lax.axis_index("dp")
    core = t + 1 - 2 * (t % 2)
    far = (t + 2) % 4
    fcore = (core + 2) % 4
    here = t // 2
    there = 1 - here
    own = pl.ds(pl.multiple_of(t * rows, rows), rows)

    loads = [
        pltpu.make_async_copy(src, dst, load_s.at[n])
        for n, (src, dst) in enumerate(
            ((wt_hbm, wt_ref), (wq_hbm, wq_ref), (wo_hbm, wo_ref), (w1_hbm, w1_ref), (w2_hbm, w2_ref))
        )
    ]
    for load in loads:
        load.start()

    barrier = pltpu.get_barrier_semaphore()
    for peer in ({"tensor": core}, {"tensor": far}, {"tensor": fcore}, {"section": 1 - s}):
        pl.semaphore_signal(barrier, inc=1, device_id=peer, device_id_type=MESH)

    def greet(j, carry):
        pl.semaphore_signal(barrier, inc=1, device_id={"dp": (z + j) % ring}, device_id_type=MESH)
        return carry

    lax.fori_loop(1, ring, greet, 0)
    pl.semaphore_wait(barrier, 3 + ring)

    def rows_of(owner):
        return pl.ds(pl.multiple_of(owner * rows, rows), rows)

    def half_of(half):
        return pl.ds(pl.multiple_of(half * half_rows, half_rows), half_rows)

    def ag_copy(k, i, which):
        owner, to = ((t, core), (t, far), (far, core))[which]
        ref = gath.at[k, i, rows_of(owner), :]
        return pltpu.make_async_remote_copy(
            src_ref=ref, dst_ref=ref, send_sem=ag_s.at[k, i, which], recv_sem=ag_r.at[k, i, which],
            device_id={"tensor": to}, device_id_type=MESH,
        )

    def ag_start(k, i):
        ag_copy(k, i, 1).start()
        ag_copy(k, i, 0).start()

    def ag_near(k, i):
        ag_copy(k, i, 0).wait_recv()

    def ag_pass(k, i):
        ag_copy(k, i, 1).wait_recv()
        ag_copy(k, i, 2).start()

    def ag_rest(k, i):
        ag_copy(k, i, 2).wait_recv()

    def ag_done(k, i):
        for which in range(3):
            ag_copy(k, i, which).wait_send()

    def rs_copy(k, i, which):
        if which < 2:
            src, dst, to = snd_c.at[k % 2, i, which], rcv_c.at[k % 2, i, which], core
        else:
            src, dst, to = snd_y.at[k % 2, i], rcv_y.at[k % 2, i], far
        return pltpu.make_async_remote_copy(
            src_ref=src, dst_ref=dst, send_sem=rs_s.at[k, i, which], recv_sem=rs_r.at[k, i, which],
            device_id={"tensor": to}, device_id_type=MESH,
        )

    mine = pl.ds(pl.multiple_of((t % 2) * rows, rows), rows)
    other = pl.ds(pl.multiple_of((1 - t % 2) * rows, rows), rows)

    def rs_give(k, i, which, part):
        keep[i, which] = part
        snd_c[k % 2, i, which] = keep[i, which, other, :].astype(BF16)
        rs_copy(k, i, which).start()

    def rs_pass(k, i):
        rs_copy(k, i, 0).wait_recv()
        snd_y[k % 2, i] = (keep[i, 0, mine, :] + rcv_c[k % 2, i, 0].astype(F32)).astype(BF16)
        rs_copy(k, i, 2).start()

    def rs_take(k, i):
        rs_copy(k, i, 1).wait_recv()
        near = keep[i, 1, mine, :] + rcv_c[k % 2, i, 1].astype(F32)
        rs_copy(k, i, 2).wait_recv()
        return near + rcv_y[k % 2, i].astype(F32)

    def rs_done(k, i):
        for which in range(3):
            rs_copy(k, i, which).wait_send()

    def sec_copy(j, src, dst):
        return lambda i: pltpu.make_async_remote_copy(
            src_ref=src.at[i], dst_ref=dst.at[i], send_sem=sec_s.at[j, i], recv_sem=sec_r.at[j, i],
            device_id={"section": 1 - s}, device_id_type=MESH,
        )

    mid_copy = sec_copy(0, mid, xin)
    grad_copy = sec_copy(1, ig_ref, gin)
    out_copy = sec_copy(2, out_ref, out_ref)

    def tiny_copy(n, j):
        ref = (emb_ref, tok_ref)[n]
        return pltpu.make_async_remote_copy(
            src_ref=ref.at[z], dst_ref=ref.at[z], send_sem=ti_s.at[n, j], recv_sem=ti_r.at[n, j],
            device_id={"dp": (z + j) % ring}, device_id_type=MESH,
        )

    def over_ring(body):
        def run(j, carry):
            body(j)
            return carry

        lax.fori_loop(1, ring, run, 0)

    def small_copy(n, j):
        return pltpu.make_async_remote_copy(
            src_ref=tiny_s.at[n], dst_ref=small_r.at[n, j], send_sem=sm_s.at[n, j], recv_sem=sm_r.at[n, j],
            device_id={"tensor": (core, far, fcore)[j]}, device_id_type=MESH,
        )

    def chain_copy(w, b, right):
        slot = b if right else b + (ring - b) * ((b + 1) // z)
        return pltpu.make_async_remote_copy(
            src_ref=partial.at[w, b], dst_ref=arrived.at[w, slot], send_sem=ch_s.at[w, b],
            recv_sem=ch_r.at[w, slot], device_id={"dp": z + 1 if right else z - 1}, device_id_type=MESH,
        )

    def arrival(w, slot):
        ref = arrived.at[w, slot]
        return pltpu.make_async_remote_copy(
            src_ref=partial.at[w, 0], dst_ref=ref, send_sem=ch_s.at[w, 0], recv_sem=ch_r.at[w, slot],
            device_id={"dp": (z + 1) % ring}, device_id_type=MESH,
        )

    flip = (2 * z) // ring

    def by_distance(body):
        def run(j, carry):
            body(flip * j + (1 - flip) * (blocks - 1 - j))
            return carry

        lax.fori_loop(0, blocks, run, 0)

    def give_blocks(w, block_of):
        def one(b):
            parts[w, b] = block_of(pl.ds(pl.multiple_of(b * cut, cut), cut))
            if chained:

                @pl.when((z == 0) & (b > 0))
                def _():
                    chain_copy(w, b, True).start()

                @pl.when((z == ring - 1) & (b < ring - 1))
                def _():
                    chain_copy(w, b, False).start()

        by_distance(one)

    def relay(w):
        def one(b):
            def add():
                arrival(w, b).wait_recv()
                partial[w, b] = (partial[w, b].astype(F32) + arrived[w, b].astype(F32)).astype(BF16)

            @pl.when((z > 0) & (b > z))
            def _():
                add()
                chain_copy(w, b, True).start()

            @pl.when((z < ring - 1) & (b < z))
            def _():
                add()
                chain_copy(w, b, False).start()

        by_distance(one)

    def settle(w):
        tot_ref[w] = partial[w, z]

        @pl.when(z > 0)
        def _():
            arrival(w, z).wait_recv()
            tot_ref[w] = (tot_ref[w].astype(F32) + arrived[w, z].astype(F32)).astype(BF16)

        @pl.when(z < ring - 1)
        def _():
            arrival(w, ring).wait_recv()
            tot_ref[w] = (tot_ref[w].astype(F32) + arrived[w, ring].astype(F32)).astype(BF16)

    def chain_done(w):
        def one(b):
            @pl.when(b > z)
            def _():
                chain_copy(w, b, True).wait_send()

            @pl.when(b < z)
            def _():
                chain_copy(w, b, False).wait_send()

        by_distance(one)

    def turn(k, n):
        for i in range(count):
            turned[n, :, i * seq : (i + 1) * seq] = gath[k, i].T

    def each_image(body):
        def run(i, carry):
            body(i)
            return carry

        lax.fori_loop(0, count, run, 0)

    def norm(x, which, i):
        mean = jnp.mean(x, axis=-1, keepdims=True)
        centre = x - mean
        root = lax.rsqrt(jnp.mean(centre * centre, axis=-1, keepdims=True) + EPS)
        hat = centre * root
        xhat[which, i] = hat
        inv[which, i] = jnp.broadcast_to(root, (rows, 128))
        return (hat * gain_ref[which : which + 1, :] + shift_ref[which : which + 1, :]).astype(BF16)

    def norm_back(da, which, i):
        hat = xhat[which, i]
        tiny_s[0, which : which + 1, :] += jnp.sum(da * hat, axis=0, keepdims=True)
        tiny_s[0, 2 + which : 3 + which, :] += jnp.sum(da, axis=0, keepdims=True)
        dhat = da * gain_ref[which : which + 1, :]
        m1 = jnp.mean(dhat, axis=-1, keepdims=True)
        m2 = jnp.mean(dhat * hat, axis=-1, keepdims=True)
        return inv[which, i][:, :1] * (dhat - m1 - hat * m2)

    tiny_s[...] = jnp.zeros_like(tiny_s)
    tok_ref[z] = jnp.zeros_like(tok_ref[z])
    emb_ref[z] = jnp.zeros_like(emb_ref[z])
    emb_ref[z, :count, :] = temb_ref[...].astype(F32)
    over_ring(lambda j: tiny_copy(0, j).start())

    @pl.when(s == 1)
    def _():
        def begin(i):
            gath[DMLP, i, own, :] = cot_ref[i]
            ag_start(DMLP, i)

        each_image(begin)

    def take_input(i):
        @pl.when(s == 0)
        def _():
            xin[i] = x_ref[i]

        @pl.when(s == 1)
        def _():
            mid_copy(i).wait_recv()

        gath[ATT, i, own, :] = norm(xin[i].astype(F32), 0, i)
        ag_start(ATT, i)

    lane = lax.broadcasted_iota(jnp.int32, (1, 2 * seq), 1)

    def tables():
        valid = lane < (2 * grid - 1) * grid
        slab = pltpu.roll(wider(rel_ref[:grid, :], 2 * seq), grid * (grid - 1), 1)
        for k in range(grid - 1):
            r = grid - 1 - k
            block = only(rel_ref[r * grid : (r + 1) * grid, :128], 0, grid)
            slab += pltpu.roll(wider(block, 2 * seq), k * grid, 1)
        none = jnp.full((1, 2 * seq), -1, jnp.int32)
        before = none
        for c in range(1, grid):
            moved = pltpu.roll(slab[c : c + 1, :], grid - c, 1)
            before = jnp.where((lane % grid == grid - c) & valid, moved, before)
        order = jnp.concatenate([jnp.where(valid, slab[:1, :], none), before], axis=1)
        step = 128
        for r in range(0, chosen.shape[0], step):
            bucket = r + lax.broadcasted_iota(jnp.int32, (step, 4 * seq), 0)
            chosen[r : r + step, :] = jnp.where(bucket == order, 1.0, 0.0).astype(BF16)
        tab[...] = jnp.zeros_like(tab)
        tab[:heads, : tab_ref.shape[1]] = tab_ref[...]
        found = add_thirds(mm(in_thirds(tab[...]), chosen[...]))
        after, before = found[:, : 2 * seq], found[:, 2 * seq :]
        for c in range(grid):
            low = pltpu.roll(after, c, 1) if c else after
            high = pltpu.roll(before, 2 * seq - (grid - c), 1)
            row = jnp.where(lane % grid >= c, low, high)
            for h in range(heads):
                tx_ref[h, c : c + 1, :] = row[h : h + 1, :]

        def expand(h, carry):
            for r in range(grid):
                shift = (2 * seq - grid * (grid - 1 - r)) % (2 * seq)
                bias[h, r * grid : (r + 1) * grid, :] = pltpu.roll(tx_ref[h], shift, 1)[:, :seq]
            return carry

        lax.fori_loop(0, heads, expand, 0)
        loads[0].wait()
        tp_ref[...] = jnp.zeros_like(tp_ref)
        emb = jnp.concatenate([temb_ref[...], jnp.zeros((16 - count, width), BF16)], axis=0)
        for c in range(3):
            tp_ref[c] = mm_nt(emb, wt_ref[c * local : (c + 1) * local, :])

    @pl.when(s == 1)
    def _():
        tables()
        each_image(lambda i: ag_pass(DMLP, i))

    each_image(take_input)

    @pl.when(s == 0)
    def _():
        tables()

    loads[1].wait()
    loads[2].wait()

    def project(i, half):
        a = gath[ATT, i, half_of(half), :]
        for c in range(3):
            part = mm_nt(a, wq_ref[c * local : (c + 1) * local, :])
            qkv[c, i, half_of(half), :] = (part + tp_ref[c, pl.ds(i, 1), :]).astype(BF16)

    def att_near(i):
        ag_near(ATT, i)
        project(i, here)

    each_image(att_near)

    def att_rest(i):
        ag_pass(ATT, i)
        ag_rest(ATT, i)
        project(i, there)
        acc[0] = jnp.zeros_like(acc[0])
        for h, (lo, hi, start, stop) in enumerate(windows):
            q = only(qkv[0, i, :, lo:hi], start, stop)
            scores = mm_nt(q, qkv[1, i, :, lo:hi]) * scale + bias[h]
            top = jnp.max(scores, axis=-1, keepdims=True)
            expo = jnp.exp(scores - top)
            p = expo / jnp.sum(expo, axis=-1, keepdims=True)
            prob[i, h] = p
            acc[0, :, lo:hi] += mm(p.astype(BF16), only(qkv[2, i, :, lo:hi], start, stop))
        att[i] = acc[0, :, :local].astype(BF16)
        far_att[i] = pltpu.roll(acc[0], far_att.shape[-1] - local, 1).astype(BF16)
        rs_give(ATT, i, 0, mm(att[i, half_of(there), :], wo_ref[...]))
        rs_give(ATT, i, 1, mm(att[i, half_of(here), :], wo_ref[...]))
        rs_pass(ATT, i)

    each_image(att_rest)

    def att_end(i):
        y = xin[i].astype(F32) + rs_take(ATT, i)
        ymid[i] = y
        gath[MLP, i, own, :] = norm(y, 1, i)
        ag_start(MLP, i)

    each_image(att_end)

    loads[3].wait()
    loads[4].wait()

    def mlp_half(i, half, which):
        a = gath[MLP, i, half_of(half), :]
        v = mm(a, w1_ref[...])
        th = jnp.tanh(GELU_A * (v + GELU_B * (v * v * v)))
        up = 0.5 * (1.0 + th)
        act[i, half_of(half), :] = (v * up).astype(BF16)
        dgel[i, half_of(half), :] = up + (0.5 * GELU_A) * v * (1.0 - th * th) * (
            1.0 + (3.0 * GELU_B) * (v * v)
        )
        rs_give(MLP, i, which, mm(act[i, half_of(half), :], w2_ref[...]))

    def mlp_near(i):
        ag_near(MLP, i)
        mlp_half(i, here, 1)

    each_image(mlp_near)

    def mlp_rest(i):
        ag_pass(MLP, i)
        ag_rest(MLP, i)
        mlp_half(i, there, 0)
        rs_pass(MLP, i)

    each_image(mlp_rest)

    tokens = count * seq

    def give_fc2():
        turn(DMLP, 0)
        give_blocks(0, lambda at: mm(turned[0, at, :], act[...].reshape(tokens, -1)).astype(BF16))

    @pl.when(s == 1)
    def _():
        each_image(lambda i: (ag_near(DMLP, i), ag_rest(DMLP, i)))
        give_fc2()

    def mlp_end(i):
        mid[i] = (ymid[i] + rs_take(MLP, i)).astype(BF16)

        @pl.when(s == 0)
        def _():
            mid_copy(i).start()

        @pl.when(s == 1)
        def _():
            out_ref[i] = mid[i]
            out_copy(i).start()

    each_image(mlp_end)

    def take_grad(i):
        mid_copy(i).wait_send()
        grad_copy(i).wait_recv()
        gath[DMLP, i, own, :] = gin[i]
        ag_start(DMLP, i)

    @pl.when(s == 0)
    def _():
        each_image(take_grad)

    @pl.when(s == 1)
    def _():
        def keep_cot(i):
            gin[i] = cot_ref[i]

        each_image(keep_cot)

    def dmlp_half(i, half, which):
        dact = mm_nt(gath[DMLP, i, half_of(half), :], w2_ref[...])
        dh[i, half_of(half), :] = (dact * dgel[i, half_of(half), :]).astype(BF16)
        rs_give(DMLP, i, which, mm_nt(dh[i, half_of(half), :], w1_ref[...]))

    def dmlp_near(i):
        rs_done(ATT, i)

        @pl.when(s == 0)
        def _():
            ag_near(DMLP, i)

        dmlp_half(i, here, 1)

    each_image(dmlp_near)

    def dmlp_rest(i):
        @pl.when(s == 0)
        def _():
            ag_pass(DMLP, i)
            ag_rest(DMLP, i)

        dmlp_half(i, there, 0)
        rs_pass(DMLP, i)

    each_image(dmlp_rest)

    turn(MLP, 1)
    give_blocks(1, lambda at: mm(turned[1, at, :], dh[...].reshape(tokens, -1)).astype(BF16))

    def dmlp_end(i):
        grad = gin[i].astype(F32) + norm_back(rs_take(DMLP, i), 1, i)
        dy1[i] = grad
        gath[DATT, i, own, :] = grad.astype(BF16)
        ag_start(DATT, i)

    each_image(dmlp_end)

    @pl.when(s == 0)
    def _():
        give_fc2()

    def datt_part(i, half):
        datt[i, half_of(half), :] = mm_nt(gath[DATT, i, half_of(half), :], wo_ref[...]).astype(BF16)

    def datt_near(i):
        rs_done(MLP, i)
        ag_near(DATT, i)
        datt_part(i, here)

    each_image(datt_near)

    def datt_rest(i):
        ag_pass(DATT, i)
        ag_rest(DATT, i)
        datt_part(i, there)
        acc[...] = jnp.zeros_like(acc)
        for h, (lo, hi, start, stop) in enumerate(windows):
            q = only(qkv[0, i, :, lo:hi], start, stop)
            k = only(qkv[1, i, :, lo:hi], start, stop)
            d = only(datt[i, :, lo:hi], start, stop)
            p = prob[i, h]
            dp = mm_nt(d, qkv[2, i, :, lo:hi])
            inner = jnp.sum(p * dp, axis=-1, keepdims=True)
            ds = (p * (dp - inner)).astype(BF16)

            @pl.when(i == 0)
            def _():
                bias[h] = ds.astype(F32)

            @pl.when(i > 0)
            def _():
                bias[h] += ds.astype(F32)

            acc[0, :, lo:hi] += mm(ds, k)
            acc[1, :, lo:hi] += mm_tn(ds, q)
            acc[2, :, lo:hi] += mm_tn(p.astype(BF16), d)
        total = jnp.zeros((seq, lanes), F32)
        for c, by in enumerate((scale, scale, 1.0)):
            lo = c * local // 128 * 128
            moved = acc[c] * by
            if c * local > lo:
                moved = pltpu.roll(moved, c * local - lo, 1)
            pieces = [jnp.zeros((seq, lo), F32)] * (lo > 0) + [moved]
            if lo + moved.shape[1] < lanes:
                pieces.append(jnp.zeros((seq, lanes - lo - moved.shape[1]), F32))
            total += jnp.concatenate(pieces, axis=1)
        dqkv[i] = total.astype(BF16)
        tok_ref[z, pl.ds(i, 1), :lanes] = jnp.sum(dqkv[i].astype(F32), axis=0, keepdims=True)
        for which, half in ((0, there), (1, here)):
            rs_give(DATT, i, which, mm(dqkv[i, half_of(half), : 3 * local], wq_ref[...]))
        rs_pass(DATT, i)

    each_image(datt_rest)

    turn(ATT, 0)
    turn(DATT, 1)

    def rest_block(at):
        first = mm(turned[0, at, :], dqkv[...].reshape(tokens, lanes))
        last = mm(turned[1, at, :], far_att[...].reshape(tokens, -1))
        seam = width - last.shape[1]
        over = lanes - seam
        return jnp.concatenate(
            [first[:, :seam], first[:, seam:] + last[:, :over], last[:, over:]], axis=1
        ).astype(BF16)

    give_blocks(2, rest_block)

    def datt_end(i):
        grad = dy1[i] + norm_back(rs_take(DATT, i), 0, i)
        ig_ref[i] = grad.astype(BF16)

        @pl.when(s == 1)
        def _():
            grad_copy(i).start()

    each_image(datt_end)

    for j in range(3):
        small_copy(0, j).start()

    def fold(h, carry):
        total = jnp.zeros((grid, 2 * seq), F32)
        for r in range(grid):
            part = wider(bias[h, r * grid : (r + 1) * grid, :], 2 * seq)
            shift = grid * (grid - 1 - r)
            total += part if shift == 0 else pltpu.roll(part, shift, 1)
        after = total[:1, :]
        before = jnp.zeros((1, 2 * seq), F32)
        for c in range(1, grid):
            row = total[c : c + 1, :]
            late = lane % grid >= c
            after += pltpu.roll(jnp.where(late, row, 0.0), 2 * seq - c, 1)
            before += pltpu.roll(jnp.where(late, 0.0, row), grid - c, 1)
        tok_ref[z, pl.ds(count + h, 1), : 4 * seq] = jnp.concatenate([after, before], axis=1)
        return carry

    lax.fori_loop(0, heads, fold, 0)
    for j in range(3):
        small_copy(0, j).wait_recv()
    over_tensor = tiny_s[0] + small_r[0, 0] + small_r[0, 1] + small_r[0, 2]
    row = lax.broadcasted_iota(jnp.int32, over_tensor.shape, 0)
    tok_ref[z, count + heads : count + heads + 1, :] = jnp.sum(
        jnp.where(row == t, over_tensor, 0.0), axis=0, keepdims=True
    )
    over_ring(lambda j: tiny_copy(1, j).start())
    if chained:
        for w in range(3):
            relay(w)
        settle(0)
    over_ring(lambda j: tiny_copy(1, j).wait_recv())

    def add_slot(j, total):
        return total + tok_ref[j]

    total = lax.fori_loop(0, ring, add_slot, jnp.zeros(tok_ref.shape[1:], F32))
    tiny_s[1] = total
    tab[...] = jnp.zeros_like(tab)
    tab[:heads, :] = tiny_s[1, count : count + heads, : 4 * seq]
    found = add_thirds(mm_nt(in_thirds(tab[...]), chosen[...]))
    gtab_ref[...] = found[:heads, : gtab_ref.shape[1]]
    for j in range(3):
        small_copy(1, j).start()
    for w in (1, 2) if chained else ():
        settle(w)
    for j in range(3):
        small_copy(1, j).wait_recv()
    last = count + heads
    small_ref[pl.ds(t, 1), :] = tiny_s[1, last : last + 1, :]
    for j, owner in enumerate((core, far, fcore)):
        small_ref[pl.ds(owner, 1), :] = small_r[1, j, last : last + 1, :]

    def finish(i):
        for k in range(4):
            ag_done(k, i)
        rs_done(DMLP, i)
        rs_done(DATT, i)

        @pl.when(s == 0)
        def _():
            out_copy(i).wait_recv()

        @pl.when(s == 1)
        def _():
            out_copy(i).wait_send()
            grad_copy(i).wait_send()

    each_image(finish)

    def tiny_left(j):
        tiny_copy(0, j).wait_recv()
        tiny_copy(0, j).wait_send()
        tiny_copy(1, j).wait_send()

    over_ring(tiny_left)
    for j in range(3):
        small_copy(0, j).wait_send()
        small_copy(1, j).wait_send()
    if chained:
        for w in range(3):
            chain_done(w)


def run_block(x, cot, wq, wt, wo, w1, w2, temb, gain, shift, rel, table, ring):
    count, rows, width = x.shape
    seq = rel.shape[0]
    heads = table.shape[0]
    local = wo.shape[0]
    hidden = w1.shape[1]
    chained = width // ring % 16 == 0
    blocks = ring if chained else 4
    cut = width // blocks
    padded = -(-local // 128) * 128
    lanes = -(-3 * local // 128) * 128
    dims = (count, rows, seq, heads, ring, chained)
    total = (3, cut, width) if chained else (3, blocks, cut, width)
    out_shape = [
        jax.ShapeDtypeStruct((count, rows, width), BF16),
        jax.ShapeDtypeStruct((count, rows, width), BF16),
        jax.ShapeDtypeStruct(total, BF16),
        jax.ShapeDtypeStruct((ring, 8, width), F32),
        jax.ShapeDtypeStruct((ring, 8, width), F32),
        jax.ShapeDtypeStruct(table.shape, F32),
        jax.ShapeDtypeStruct((4, width), F32),
    ]
    vm = pltpu.VMEM
    dma = pltpu.SemaphoreType.DMA
    scratch = [
        vm(wq.shape, BF16),
        vm(wt.shape, BF16),
        vm(wo.shape, BF16),
        vm(w1.shape, BF16),
        vm(w2.shape, BF16),
        vm((3, 16, local), F32),
        vm((heads, int(round(seq**0.5)), 2 * seq), F32),
        vm((4 * seq, 4 * seq), BF16),
        vm((16, 4 * seq), F32),
        vm((3, blocks, cut, width) if chained else (16, 128), BF16),
        vm((3, blocks + 1, cut, width) if chained else (16, 128), BF16),
        vm((2, 8, width), F32),
        vm((2, 3, 8, width), F32),
        vm((count, rows, width), BF16),
        vm((count, rows, width), BF16),
        vm((count, rows, width), BF16),
        vm((4, count, seq, width), BF16),
        vm((count, 2, 2 * rows, width), F32),
        vm((2, count, 2, rows, width), BF16),
        vm((2, count, rows, width), BF16),
        vm((2, count, 2, rows, width), BF16),
        vm((2, count, rows, width), BF16),
        vm((heads, seq, seq), F32),
        vm((count, heads, seq, seq), F32),
        vm((3, count, seq, local), BF16),
        vm((count, seq, local), BF16),
        vm((count, seq, hidden), BF16),
        vm((count, seq, hidden), F32),
        vm((2, count, rows, width), F32),
        vm((2, count, rows, 128), F32),
        vm((count, rows, width), F32),
        vm((count, rows, width), F32),
        vm((count, seq, lanes), BF16),
        vm((count, seq, hidden), BF16),
        vm((count, seq, local), BF16),
        vm((3, seq, padded), F32),
        vm((2, width, count * seq), BF16),
        vm((count, seq, padded), BF16),
        dma((5,)),
        dma((4, count, 3)),
        dma((4, count, 3)),
        dma((4, count, 3)),
        dma((4, count, 3)),
        dma((3, count)),
        dma((3, count)),
        dma((3, blocks)),
        dma((3, blocks + 1)),
        dma((2, ring)),
        dma((2, ring)),
        dma((2, 3)),
        dma((2, 3)),
    ]
    whole = pl.BlockSpec(memory_space=pltpu.VMEM)
    lies = pl.BlockSpec(memory_space=pl.ANY)
    return pl.pallas_call(
        functools.partial(block_kernel, dims),
        out_shape=out_shape,
        in_specs=[whole] * 2 + [lies] * 5 + [whole] * 5,
        out_specs=[whole] * len(out_shape),
        scratch_shapes=scratch,
        compiler_params=pltpu.CompilerParams(
            collective_id=0, has_side_effects=True, vmem_limit_bytes=63 * 2**20
        ),
        name="blocks",
    )(x, cot, wq, wt, wo, w1, w2, temb, gain, shift, rel, table)


def per_device(
    images, timesteps, t_table, rel_index, w_qkv, w_time, w_out, w_fc1, w_fc2, rel_table,
    norm_gain, norm_shift, cotangent,
):
    ring = lax.axis_size("dp")
    count = images.shape[0]
    width = images.shape[-1]
    local = w_out.shape[1]
    cut = width // ring
    embedded = t_table[timesteps]
    wq = jnp.transpose(w_qkv[0], (1, 2, 0)).reshape(3 * local, width)
    wt = jnp.transpose(w_time[0], (1, 2, 0)).reshape(3 * local, width)
    output, in_grad, total, sums, emb, g_table, small = run_block(
        images, cotangent, wq, wt, w_out[0], w_fc1[0], w_fc2[0], embedded, norm_gain[0], norm_shift[0],
        rel_index, rel_table[0].T, ring,
    )
    if total.ndim == 4:
        total = lax.psum_scatter(
            total.reshape(3, width, width), "dp", scatter_dimension=1, tiled=True
        )
    total = total.astype(F32)
    g_fc2 = total[0].T
    g_fc1 = total[1]
    g_qkv = total[2, :, : 3 * local].reshape(cut, 3, local)
    g_out = total[2, :, 3 * local :].T
    sums = sums[:, :count, : 3 * local].reshape(ring * count, 3, local)
    emb = emb[:, :count].reshape(ring * count, width)
    emb = lax.dynamic_slice_in_dim(emb, lax.axis_index("dp") * cut, cut, axis=1)
    g_time = jnp.einsum("id,icj->dcj", emb, sums, precision=lax.Precision.HIGHEST)
    return (
        output, in_grad[None], g_qkv[None], g_time[None], g_out[None], g_fc1[None], g_fc2[None],
        g_table.T[None], small[None, :2], small[None, 2:],
    )


def solution(mesh):
    in_specs = (
        P("dp", "tensor", None),
        P("dp"),
        P(),
        P(),
        P("section", None, None, "tensor"),
        P("section", None, None, "tensor"),
        P("section", "tensor", None),
        P("section", None, "tensor"),
        P("section", "tensor", None),
        P("section", None, "tensor"),
        P("section", None, None),
        P("section", None, None),
        P("dp", "tensor", None),
    )
    out_specs = (
        P("dp", "tensor", None),
        P("section", "dp", "tensor", None),
        P("section", "dp", None, "tensor"),
        P("section", "dp", None, "tensor"),
        P("section", "tensor", "dp"),
        P("section", "dp", "tensor"),
        P("section", "tensor", "dp"),
        P("section", None, "tensor"),
        P("section", None, None),
        P("section", None, None),
    )
    return jax.shard_map(
        per_device, mesh=mesh, in_specs=in_specs, out_specs=out_specs, check_vma=False
    )
```

time: 385 us -> 303 us (0.79)
  Pallas kernels: 161 us -> 278 us
  blocking collectives: 100 us -> 0 us
  waiting for transfers between devices: 77.6 us -> 0 us
  between operations: 14 us -> 0.7 us
  other arithmetic: 8.13 us -> 2.48 us
    pallas_call x1, Pallas kernels: 161 us -> 278 us  [run_block(): pl.pallas_call(functools.partial(block_kernel, dims), out_shape=out_shape...]
    psum x2 -> x0, blocking collectives: 76.8 us -> none  [the longest x1 61.1 us: per_device(): small = lax.psum(small, ('tensor', 'dp'))]
    reduce_scatter x4 -> x0, waiting for transfers between devices: 75.7 us -> none  [scatter(): lax.psum_scatter(grad, 'dp', scatter_dimension=axis, tiled=True).astype(F32)]
    all_gather x2 -> x0, blocking collectives: 23.5 us -> none  [the longest x1 12.3 us: per_device(): all_sums = lax.all_gather(tok, 'dp', axis=0, tiled=True)]
    broadcast_in_dim x4 -> x0, other arithmetic: 7.68 us -> none  [the longest x1 2.24 us: per_device(): g_qkv = jnp.transpose(scatter(gq, 1), (1, 0, 2))[None]]
    reshape x6 -> x2, local copies, waits for them, and re-layouts: 4.9 us -> 0.14 us  [the longest x1 0.11 us: per_device(): sums = sums[:, :count, :3 * local].reshape(ring * count, 3, local)]
    slice x3 -> x5, local copies, waits for them, and re-layouts: 1.28 us -> 5.65 us  [the longest x2 2.67 us: per_device(): g_qkv = total[2, :, :3 * local].reshape(cut, 3, local)]
  transfers between devices with their start and end apart: 4 -> 0, of which waited for: 2 -> 0; matrix products, arithmetic and copies ran while one was open for 3% -> 0% of each run, Pallas kernels for 0% -> 0%
where the time goes in v3:
time: 303 us; the launch traced here: 300 us
  Pallas kernels  278 us (92%)
  local copies, waits for them, and re-layouts  15.4 us (5%)
    pallas_call x1, Pallas kernels, run_block(): pl.pallas_call(functools.partial(block_kernel, dims), out_shape=out_shape...  278 us

profile of v3, /device:TPU:9, one launch (start us, length us, event | category | flops | bytes accessed | tf_op | source)
XLA Modules:
  0.0 299.5 jit_solution(18350672448342844342)
XLA Ops:
  0.6 0.7 compare_select_fusion
  1.3 3.1 %gather_fusion = bf16[2,1152]{1,0:T(2,128)(2,1)} fusion(bf16[1000,1152]{1,0:T(8,128)(2,1)} %param.15, s32[1024]{0:T(1024)S(1)} %pad_clamp_fusion), kind=kCustom, calls=%fused_computation | custom fusion | bytes 9224 | tf_op jit(solution)/shard_map/gather | solution.py:819
  4.4 278.5 %blocks.1 = (bf16[2,64,1152]{2,1,0:T(8,128)(2,1)}, bf16[2,64,1152]{2,1,0:T(8,128)(2,1)}, bf16[3,288,1152]{2,1,0:T(8,128)(2,1)}, f32[4,8,1152]{2,1,0:T(8,128)}, f...) custom-call(bf16[2,64,1152]{2,1,0:T(8,128)(2,1)} %x_ref.1, bf16[2,64,1152]{2,1,0:T(8,128)(2,1)} %cot_ref.1, ...), custom_call_target="tpu_custom_call" | custom-call | tf_op jit(solution)/shard_map/blocks/pallas_call | solution.py:797
  282.9 0.9 slice.26
  283.8 0.1 reshape.35
  283.9 0.9 slice.25
  284.9 2.4 convolution_bitcast_fusion
  287.3 1.8 convert_element_type.3
  289.1 0.0 copy-start
  289.1 1.1 slice_bitcast_fusion
  290.3 0.2 slice_bitcast_fusion.1
  290.5 1.0 copy.29
  291.5 0.0 copy-done
  291.5 1.0 slice.34
  292.5 1.6 copy.26
  294.1 1.6 copy.28
  295.7 0.0 copy-start.3
  295.7 0.0 copy-start.2
  295.7 0.0 copy-start.1
  295.7 0.0 copy-start.4
  295.7 1.1 slice.36
  296.9 0.0 copy-done.3
  296.9 0.6 slice_bitcast_fusion.2
  297.5 0.0 copy-done.2
  297.5 0.7 copy.35
  298.2 0.0 copy-done.1
  298.2 0.7 copy.36
  298.9 0.0 copy-done.4
  298.9 0.6 copy.37
  (2 shorter events, 0.0 us)
Async XLA Ops:
  289.1 2.3 copy-start
  295.7 1.2 copy-start.3
  295.7 1.8 copy-start.2
  295.7 2.5 copy-start.1
  295.7 3.2 %copy-start.4 = (f32[4,961]{1,0:T(4,128)S(1)}, f32[4,961]{1,0:T(4,128)}, u32[]{:S(2)}) copy-start(f32[4,961]{1,0:T(4,128)} %get-tuple-element.22) | copy-start | bytes 46132

commit v4 on v3

--- a/solution.py
+++ b/solution.py
@@ -64,11 +64,11 @@
     cfg,
     x_ref, cot_ref, wq_hbm, wt_hbm, wo_hbm, w1_hbm, w2_hbm, temb_ref, gain_ref, shift_ref, rel_ref, tab_ref,
     out_ref, ig_ref, tot_ref, tok_ref, emb_ref, gtab_ref, small_ref,
-    wq_ref, wt_ref, wo_ref, w1_ref, w2_ref, tp_ref, tx_ref, chosen, tab, partial, arrived,
+    wq_ref, spare, wo_ref, w1_ref, w2_ref, tp_ref, tx_ref, chosen, tab, partial, arrived,
     tiny_s, small_r,
     xin, gin, mid, gath, keep, rcv_c, rcv_y, snd_c, snd_y, bias, prob, qkv, att, act, dgel,
-    xhat, inv, ymid, dy1, dqkv, dh, datt, acc, turned, far_att,
-    load_s, ag_s, ag_r, rs_s, rs_r, sec_s, sec_r, ch_s, ch_r, ti_s, ti_r, sm_s, sm_r,
+    xhat, inv, ymid, dqkv, dh, datt, acc, turned, far_att, act2, dh2, dqkv2, far_att2,
+    load_s, ag_s, ag_r, rs_s, rs_r, sec_s, sec_r, ch_s, ch_r, fac_s, fac_r, ti_s, ti_r, sm_s, sm_r,
 ):
     count, rows, seq, heads, ring, chained = cfg
     half_rows = 2 * rows
@@ -79,8 +79,9 @@
     scale = (local // heads) ** (-0.5)
     blocks = partial.shape[1] if chained else tot_ref.shape[1]
     cut = width // blocks
+    pieces = partial.shape[2] if chained else 1
+    slim = cut // pieces
     lanes = dqkv.shape[-1]
-    parts = partial if chained else tot_ref
 
     s = lax.axis_index("section")
     t = lax.axis_index("tensor")
@@ -92,6 +93,8 @@
     there = 1 - here
     own = pl.ds(pl.multiple_of(t * rows, rows), rows)
 
+    wt_ref = partial.at[2, :3] if chained else spare
+
     loads = [
         pltpu.make_async_copy(src, dst, load_s.at[n])
         for n, (src, dst) in enumerate(
@@ -120,7 +123,7 @@
 
     def ag_copy(k, i, which):
         owner, to = ((t, core), (t, far), (far, core))[which]
-        ref = gath.at[k, i, rows_of(owner), :]
+        ref = gath.at[k % 3, i, rows_of(owner), :]
         return pltpu.make_async_remote_copy(
             src_ref=ref, dst_ref=ref, send_sem=ag_s.at[k, i, which], recv_sem=ag_r.at[k, i, which],
             device_id={"tensor": to}, device_id_type=MESH,
@@ -154,22 +157,21 @@
             device_id={"tensor": to}, device_id_type=MESH,
         )
 
-    mine = pl.ds(pl.multiple_of((t % 2) * rows, rows), rows)
-    other = pl.ds(pl.multiple_of((1 - t % 2) * rows, rows), rows)
-
     def rs_give(k, i, which, part):
-        keep[i, which] = part
-        snd_c[k % 2, i, which] = keep[i, which, other, :].astype(BF16)
+        odd = t % 2 == 1
+        low, high = part[:rows], part[rows:]
+        snd_c[k % 2, i, which] = jnp.where(odd, low, high).astype(BF16)
         rs_copy(k, i, which).start()
+        keep[i, which] = jnp.where(odd, high, low)
 
     def rs_pass(k, i):
         rs_copy(k, i, 0).wait_recv()
-        snd_y[k % 2, i] = (keep[i, 0, mine, :] + rcv_c[k % 2, i, 0].astype(F32)).astype(BF16)
+        snd_y[k % 2, i] = (keep[i, 0] + rcv_c[k % 2, i, 0].astype(F32)).astype(BF16)
         rs_copy(k, i, 2).start()
 
     def rs_take(k, i):
         rs_copy(k, i, 1).wait_recv()
-        near = keep[i, 1, mine, :] + rcv_c[k % 2, i, 1].astype(F32)
+        near = keep[i, 1] + rcv_c[k % 2, i, 1].astype(F32)
         rs_copy(k, i, 2).wait_recv()
         return near + rcv_y[k % 2, i].astype(F32)
 
@@ -207,90 +209,164 @@
             device_id={"tensor": (core, far, fcore)[j]}, device_id_type=MESH,
         )
 
-    def chain_copy(w, b, right):
-        slot = b if right else b + (ring - b) * ((b + 1) // z)
+    mate = z + 1 - 2 * (z % 2)
+    across = 3 - z
+    beyond = 3 * (2 - z)
+    is_end = (z == 0) | (z == 3)
+    is_mate = (z == 1) | (z == 2)
+
+    def factor_copy(n):
+        if n < 4:
+            src, dst = turned.at[n, t % 2], turned.at[n, count + t % 2]
+        else:
+            src, dst = ((act, act2), (dh, dh2), (dqkv, dqkv2), (far_att, far_att2))[n - 4]
         return pltpu.make_async_remote_copy(
-            src_ref=partial.at[w, b], dst_ref=arrived.at[w, slot], send_sem=ch_s.at[w, b],
-            recv_sem=ch_r.at[w, slot], device_id={"dp": z + 1 if right else z - 1}, device_id_type=MESH,
-        )
-
-    def arrival(w, slot):
-        ref = arrived.at[w, slot]
+            src_ref=src, dst_ref=dst, send_sem=fac_s.at[n], recv_sem=fac_r.at[n],
+            device_id={"dp": mate}, device_id_type=MESH,
+        )
+
+    def share_copy(k):
+        ref = turned.at[k, count + t % 2]
         return pltpu.make_async_remote_copy(
-            src_ref=partial.at[w, 0], dst_ref=ref, send_sem=ch_s.at[w, 0], recv_sem=ch_r.at[w, slot],
-            device_id={"dp": (z + 1) % ring}, device_id_type=MESH,
-        )
-
-    flip = (2 * z) // ring
-
-    def by_distance(body):
-        def run(j, carry):
-            body(flip * j + (1 - flip) * (blocks - 1 - j))
+            src_ref=ref, dst_ref=ref, send_sem=fac_s.at[8 + k], recv_sem=fac_r.at[8 + k],
+            device_id={"tensor": core}, device_id_type=MESH,
+        )
+
+    def give_factor(*which):
+        if chained:
+
+            @pl.when(is_end)
+            def _():
+                for n in which:
+                    factor_copy(n).start()
+
+    def share_factor(k):
+        if chained:
+
+            @pl.when(is_mate)
+            def _():
+                factor_copy(k).wait_recv()
+                share_copy(k).start()
+
+    def cross_copy(w, slot, c):
+        return pltpu.make_async_remote_copy(
+            src_ref=partial.at[w, (beyond, across)[slot], c], dst_ref=arrived.at[w, slot, c],
+            send_sem=ch_s.at[w, slot, c], recv_sem=ch_r.at[w, slot, c],
+            device_id={"dp": across}, device_id_type=MESH,
+        )
+
+    def home_copy(w, c):
+        return pltpu.make_async_remote_copy(
+            src_ref=partial.at[w, mate, c], dst_ref=arrived.at[w, 0, c],
+            send_sem=ch_s.at[w, 2, c], recv_sem=ch_r.at[w, 0, c],
+            device_id={"dp": mate}, device_id_type=MESH,
+        )
+
+    def each_piece(body):
+        def run(c, carry):
+            body(c)
             return carry
 
-        lax.fori_loop(0, blocks, run, 0)
-
-    def give_blocks(w, block_of):
-        def one(b):
-            parts[w, b] = block_of(pl.ds(pl.multiple_of(b * cut, cut), cut))
-            if chained:
-
-                @pl.when((z == 0) & (b > 0))
-                def _():
-                    chain_copy(w, b, True).start()
-
-                @pl.when((z == ring - 1) & (b < ring - 1))
-                def _():
-                    chain_copy(w, b, False).start()
-
-        by_distance(one)
+        lax.fori_loop(0, pieces, run, 0)
+
+    def give_blocks(w, needs, product):
+        if not chained:
+
+            def whole(b, carry):
+                tot_ref[w, b] = product(pl.ds(pl.multiple_of(b * cut, cut), cut), 0).astype(BF16)
+                return carry
+
+            lax.fori_loop(0, blocks, whole, 0)
+            return
+
+        def rows_at(b, c):
+            return pl.ds(pl.multiple_of(b * cut + c * slim, slim), slim)
+
+        def alone(b):
+            def one(c):
+                partial[w, b, c] = product(rows_at(b, c), 0).astype(BF16)
+
+            each_piece(one)
+
+        def both(b, slot=None):
+            def one(c):
+                at = rows_at(b, c)
+                partial[w, b, c] = (product(at, 0) + product(at, 1)).astype(BF16)
+                if slot is not None:
+                    cross_copy(w, slot, c).start()
+
+            each_piece(one)
+
+        @pl.when(is_end)
+        def _():
+            alone(z)
+
+        @pl.when(is_mate)
+        def _():
+            for n in needs:
+                if n < 4:
+                    share_copy(n).wait_recv()
+                else:
+                    factor_copy(n).wait_recv()
+            both(beyond, 0)
+            both(across, 1)
+            both(z)
+            alone(mate)
 
     def relay(w):
-        def one(b):
-            def add():
-                arrival(w, b).wait_recv()
-                partial[w, b] = (partial[w, b].astype(F32) + arrived[w, b].astype(F32)).astype(BF16)
-
-            @pl.when((z > 0) & (b > z))
-            def _():
-                add()
-                chain_copy(w, b, True).start()
-
-            @pl.when((z < ring - 1) & (b < z))
-            def _():
-                add()
-                chain_copy(w, b, False).start()
-
-        by_distance(one)
+        @pl.when(is_mate)
+        def _():
+            def one(c):
+                cross_copy(w, 0, c).wait_recv()
+                partial[w, mate, c] = (
+                    partial[w, mate, c].astype(F32) + arrived[w, 0, c].astype(F32)
+                ).astype(BF16)
+                home_copy(w, c).start()
+
+            each_piece(one)
 
     def settle(w):
-        tot_ref[w] = partial[w, z]
-
-        @pl.when(z > 0)
-        def _():
-            arrival(w, z).wait_recv()
-            tot_ref[w] = (tot_ref[w].astype(F32) + arrived[w, z].astype(F32)).astype(BF16)
-
-        @pl.when(z < ring - 1)
-        def _():
-            arrival(w, ring).wait_recv()
-            tot_ref[w] = (tot_ref[w].astype(F32) + arrived[w, ring].astype(F32)).astype(BF16)
-
-    def chain_done(w):
-        def one(b):
-            @pl.when(b > z)
-            def _():
-                chain_copy(w, b, True).wait_send()
-
-            @pl.when(b < z)
-            def _():
-                chain_copy(w, b, False).wait_send()
-
-        by_distance(one)
-
-    def turn(k, n):
+        def finish(slot, copy):
+            def one(c):
+                copy(c).wait_recv()
+                tot_ref[w, c] = (partial[w, z, c].astype(F32) + arrived[w, slot, c].astype(F32)).astype(BF16)
+
+            each_piece(one)
+
+        @pl.when(is_mate)
+        def _():
+            finish(1, lambda c: cross_copy(w, 1, c))
+
+        @pl.when(is_end)
+        def _():
+            finish(0, lambda c: home_copy(w, c))
+
+    def weights_left():
+        @pl.when(is_end)
+        def _():
+            for n in range(8):
+                factor_copy(n).wait_send()
+
+        @pl.when(is_mate)
+        def _():
+            for k in range(4):
+                share_copy(k).wait_send()
+            for w in range(3):
+                for c in range(pieces):
+                    cross_copy(w, 0, c).wait_send()
+                    cross_copy(w, 1, c).wait_send()
+                    home_copy(w, c).wait_send()
+
+    def turn(k):
         for i in range(count):
-            turned[n, :, i * seq : (i + 1) * seq] = gath[k, i].T
+            turned[k, i] = gath[k % 3, i].T
+
+    def product(k, mine, theirs):
+        def rows_of_product(at, side):
+            right = (mine, theirs)[side]
+            return sum(mm(turned[k, side * count + i, at, :], right[i]) for i in range(count))
+
+        return rows_of_product
 
     def each_image(body):
         def run(i, carry):
@@ -384,12 +460,20 @@
         tp_ref[...] = jnp.zeros_like(tp_ref)
         emb = jnp.concatenate([temb_ref[...], jnp.zeros((16 - count, width), BF16)], axis=0)
         for c in range(3):
-            tp_ref[c] = mm_nt(emb, wt_ref[c * local : (c + 1) * local, :])
+            tp_ref[c] = mm_nt(emb, wt_ref[c].reshape(local, width))
 
     @pl.when(s == 1)
     def _():
         tables()
-        each_image(lambda i: ag_pass(DMLP, i))
+
+        def spread_cot(i):
+            ag_pass(DMLP, i)
+            ag_near(DMLP, i)
+            ag_rest(DMLP, i)
+
+        each_image(spread_cot)
+        turn(DMLP)
+        give_factor(2)
 
     each_image(take_input)
 
@@ -433,8 +517,12 @@
 
     each_image(att_rest)
 
+    turn(ATT)
+    give_factor(0, 7)
+
     def att_end(i):
         y = xin[i].astype(F32) + rs_take(ATT, i)
+        ag_done(ATT, i)
         ymid[i] = y
         gath[MLP, i, own, :] = norm(y, 1, i)
         ag_start(MLP, i)
@@ -450,9 +538,8 @@
         th = jnp.tanh(GELU_A * (v + GELU_B * (v * v * v)))
         up = 0.5 * (1.0 + th)
         act[i, half_of(half), :] = (v * up).astype(BF16)
-        dgel[i, half_of(half), :] = up + (0.5 * GELU_A) * v * (1.0 - th * th) * (
-            1.0 + (3.0 * GELU_B) * (v * v)
-        )
+        slope = up + (0.5 * GELU_A) * v * (1.0 - th * th) * (1.0 + (3.0 * GELU_B) * (v * v))
+        dgel[i, half_of(half), :] = slope.astype(BF16)
         rs_give(MLP, i, which, mm(act[i, half_of(half), :], w2_ref[...]))
 
     def mlp_near(i):
@@ -469,16 +556,8 @@
 
     each_image(mlp_rest)
 
-    tokens = count * seq
-
-    def give_fc2():
-        turn(DMLP, 0)
-        give_blocks(0, lambda at: mm(turned[0, at, :], act[...].reshape(tokens, -1)).astype(BF16))
-
-    @pl.when(s == 1)
-    def _():
-        each_image(lambda i: (ag_near(DMLP, i), ag_rest(DMLP, i)))
-        give_fc2()
+    turn(MLP)
+    give_factor(1, 4)
 
     def mlp_end(i):
         mid[i] = (ymid[i] + rs_take(MLP, i)).astype(BF16)
@@ -538,23 +617,36 @@
 
     each_image(dmlp_rest)
 
-    turn(MLP, 1)
-    give_blocks(1, lambda at: mm(turned[1, at, :], dh[...].reshape(tokens, -1)).astype(BF16))
+    @pl.when(s == 0)
+    def _():
+        turn(DMLP)
+        give_factor(2)
+        share_factor(ATT)
+        share_factor(MLP)
+
+    give_factor(5)
 
     def dmlp_end(i):
         grad = gin[i].astype(F32) + norm_back(rs_take(DMLP, i), 1, i)
-        dy1[i] = grad
-        gath[DATT, i, own, :] = grad.astype(BF16)
+        ymid[i] = grad
+        gath[DATT % 3, i, own, :] = grad.astype(BF16)
         ag_start(DATT, i)
 
     each_image(dmlp_end)
+
+    def job_fc2():
+        give_blocks(0, (2, 4), product(DMLP, act, act2))
+
+    def job_fc1():
+        give_blocks(1, (1, 5), product(MLP, dh, dh2))
 
     @pl.when(s == 0)
     def _():
-        give_fc2()
+        share_factor(DMLP)
+        job_fc2()
 
     def datt_part(i, half):
-        datt[i, half_of(half), :] = mm_nt(gath[DATT, i, half_of(half), :], wo_ref[...]).astype(BF16)
+        datt[i, half_of(half), :] = mm_nt(gath[DATT % 3, i, half_of(half), :], wo_ref[...]).astype(BF16)
 
     def datt_near(i):
         rs_done(MLP, i)
@@ -606,22 +698,16 @@
 
     each_image(datt_rest)
 
-    turn(ATT, 0)
-    turn(DATT, 1)
-
-    def rest_block(at):
-        first = mm(turned[0, at, :], dqkv[...].reshape(tokens, lanes))
-        last = mm(turned[1, at, :], far_att[...].reshape(tokens, -1))
-        seam = width - last.shape[1]
-        over = lanes - seam
-        return jnp.concatenate(
-            [first[:, :seam], first[:, seam:] + last[:, :over], last[:, over:]], axis=1
-        ).astype(BF16)
-
-    give_blocks(2, rest_block)
+    give_factor(6)
+    turn(DATT)
+    give_factor(3)
+
+    @pl.when(s == 0)
+    def _():
+        job_fc1()
 
     def datt_end(i):
-        grad = dy1[i] + norm_back(rs_take(DATT, i), 0, i)
+        grad = ymid[i] + norm_back(rs_take(DATT, i), 0, i)
         ig_ref[i] = grad.astype(BF16)
 
         @pl.when(s == 1)
@@ -658,10 +744,35 @@
         jnp.where(row == t, over_tensor, 0.0), axis=0, keepdims=True
     )
     over_ring(lambda j: tiny_copy(1, j).start())
+
+    @pl.when(s == 1)
+    def _():
+        share_factor(DMLP)
+        share_factor(ATT)
+        share_factor(MLP)
+        job_fc2()
+        job_fc1()
+
     if chained:
-        for w in range(3):
-            relay(w)
+        relay(0)
+
+    share_factor(DATT)
+    from_qkv = product(ATT, dqkv, dqkv2)
+    from_out = product(DATT, far_att, far_att2)
+
+    def rest_product(at, side):
+        first, last = from_qkv(at, side), from_out(at, side)
+        seam = width - last.shape[1]
+        over = lanes - seam
+        return jnp.concatenate(
+            [first[:, :seam], first[:, seam:] + last[:, :over], last[:, over:]], axis=1
+        )
+
+    give_blocks(2, (0, 3, 6, 7), rest_product)
+    if chained:
+        relay(1)
         settle(0)
+        relay(2)
     over_ring(lambda j: tiny_copy(1, j).wait_recv())
 
     def add_slot(j, total):
@@ -685,7 +796,7 @@
         small_ref[pl.ds(owner, 1), :] = small_r[1, j, last : last + 1, :]
 
     def finish(i):
-        for k in range(4):
+        for k in (MLP, DMLP, DATT):
             ag_done(k, i)
         rs_done(DMLP, i)
         rs_done(DATT, i)
@@ -711,8 +822,7 @@
         small_copy(0, j).wait_send()
         small_copy(1, j).wait_send()
     if chained:
-        for w in range(3):
-            chain_done(w)
+        weights_left()
 
 
 def run_block(x, cot, wq, wt, wo, w1, w2, temb, gain, shift, rel, table, ring):
@@ -721,13 +831,17 @@
     heads = table.shape[0]
     local = wo.shape[0]
     hidden = w1.shape[1]
-    chained = width // ring % 16 == 0
-    blocks = ring if chained else 4
+    chained = ring == 4 and count == 2 and width % (16 * ring) == 0
+    blocks = 4
+    pieces = 3 if width // 4 % 48 == 0 else 1
     cut = width // blocks
+    chained = chained and local == width // 4
+    if chained:
+        wt = wt.reshape(3, pieces, local // pieces, width)
     padded = -(-local // 128) * 128
     lanes = -(-3 * local // 128) * 128
     dims = (count, rows, seq, heads, ring, chained)
-    total = (3, cut, width) if chained else (3, blocks, cut, width)
+    total = (3, pieces, cut // pieces, width) if chained else (3, blocks, cut, width)
     out_shape = [
         jax.ShapeDtypeStruct((count, rows, width), BF16),
         jax.ShapeDtypeStruct((count, rows, width), BF16),
@@ -741,7 +855,7 @@
     dma = pltpu.SemaphoreType.DMA
     scratch = [
         vm(wq.shape, BF16),
-        vm(wt.shape, BF16),
+        vm((16, 128) if chained else wt.shape, BF16),
         vm(wo.shape, BF16),
         vm(w1.shape, BF16),
         vm(w2.shape, BF16),
@@ -749,15 +863,15 @@
         vm((heads, int(round(seq**0.5)), 2 * seq), F32),
         vm((4 * seq, 4 * seq), BF16),
         vm((16, 4 * seq), F32),
-        vm((3, blocks, cut, width) if chained else (16, 128), BF16),
-        vm((3, blocks + 1, cut, width) if chained else (16, 128), BF16),
+        vm((3, blocks, pieces, cut // pieces, width) if chained else (16, 128), BF16),
+        vm((3, 2, pieces, cut // pieces, width) if chained else (16, 128), BF16),
         vm((2, 8, width), F32),
         vm((2, 3, 8, width), F32),
         vm((count, rows, width), BF16),
         vm((count, rows, width), BF16),
         vm((count, rows, width), BF16),
-        vm((4, count, seq, width), BF16),
-        vm((count, 2, 2 * rows, width), F32),
+        vm((3, count, seq, width), BF16),
+        vm((count, 2, rows, width), F32),
         vm((2, count, 2, rows, width), BF16),
         vm((2, count, rows, width), BF16),
         vm((2, count, 2, rows, width), BF16),
@@ -767,17 +881,20 @@
         vm((3, count, seq, local), BF16),
         vm((count, seq, local), BF16),
         vm((count, seq, hidden), BF16),
-        vm((count, seq, hidden), F32),
+        vm((count, seq, hidden), BF16),
         vm((2, count, rows, width), F32),
         vm((2, count, rows, 128), F32),
-        vm((count, rows, width), F32),
         vm((count, rows, width), F32),
         vm((count, seq, lanes), BF16),
         vm((count, seq, hidden), BF16),
         vm((count, seq, local), BF16),
         vm((3, seq, padded), F32),
-        vm((2, width, count * seq), BF16),
+        vm((4, 2 * count if chained else count, width, seq), BF16),
         vm((count, seq, padded), BF16),
+        vm((count, seq, hidden) if chained else (16, 128), BF16),
+        vm((count, seq, hidden) if chained else (16, 128), BF16),
+        vm((count, seq, lanes) if chained else (16, 128), BF16),
+        vm((count, seq, padded) if chained else (16, 128), BF16),
         dma((5,)),
         dma((4, count, 3)),
         dma((4, count, 3)),
@@ -785,8 +902,10 @@
         dma((4, count, 3)),
         dma((3, count)),
         dma((3, count)),
-        dma((3, blocks)),
-        dma((3, blocks + 1)),
+        dma((3, 3, pieces)),
+        dma((3, 2, pieces)),
+        dma((12,)),
+        dma((12,)),
         dma((2, ring)),
         dma((2, ring)),
         dma((2, 3)),
@@ -818,15 +937,14 @@
     cut = width // ring
     embedded = t_table[timesteps]
     wq = jnp.transpose(w_qkv[0], (1, 2, 0)).reshape(3 * local, width)
-    wt = jnp.transpose(w_time[0], (1, 2, 0)).reshape(3 * local, width)
+    wt = jnp.transpose(w_time[0], (1, 2, 0))
     output, in_grad, total, sums, emb, g_table, small = run_block(
         images, cotangent, wq, wt, w_out[0], w_fc1[0], w_fc2[0], embedded, norm_gain[0], norm_shift[0],
         rel_index, rel_table[0].T, ring,
     )
-    if total.ndim == 4:
-        total = lax.psum_scatter(
-            total.reshape(3, width, width), "dp", scatter_dimension=1, tiled=True
-        )
+    total = total.reshape(3, -1, width)
+    if total.shape[1] != cut:
+        total = lax.psum_scatter(total, "dp", scatter_dimension=1, tiled=True)
     total = total.astype(F32)
     g_fc2 = total[0].T
     g_fc1 = total[1]

time: 303 us -> 267 us (0.88)
  Pallas kernels: 278 us -> 242 us
    pallas_call x1, Pallas kernels: 278 us -> 242 us  [run_block(): pl.pallas_call(functools.partial(block_kernel, dims), out_shape=out_shape...]
    unnamed x15 -> x18, local copies, waits for them, and re-layouts: 4.61 us -> 6.9 us
where the time goes in v4:
time: 267 us; the launch traced here: 263 us
  Pallas kernels  242 us (91%)
  local copies, waits for them, and re-layouts  15.7 us (6%)
    pallas_call x1, Pallas kernels, run_block(): pl.pallas_call(functools.partial(block_kernel, dims), out_shape=out_shape...  242 us
    unnamed x18, local copies, waits for them, and re-layouts  6.9 us

profile of v4, /device:TPU:9, one launch (start us, length us, event | category | flops | bytes accessed | tf_op | source)
XLA Modules:
  0.0 263.4 jit_solution(6523507035002019835)
XLA Ops:
  0.6 0.7 compare_select_fusion
  1.3 3.1 %gather_fusion = bf16[2,1152]{1,0:T(2,128)(2,1)} fusion(bf16[1000,1152]{1,0:T(8,128)(2,1)} %param.15, s32[1024]{0:T(1024)S(1)} %pad_clamp_fusion), kind=kCustom, calls=%fused_computation | custom fusion | bytes 9224 | tf_op jit(solution)/shard_map/gather | solution.py:938
  4.4 242.0 %blocks.1 = (bf16[2,64,1152]{2,1,0:T(8,128)(2,1)}, bf16[2,64,1152]{2,1,0:T(8,128)(2,1)}, bf16[3,3,96,1152]{3,2,1,0:T(8,128)(2,1)}, f32[4,8,1152]{2,1,0:T(8,128)}...) custom-call(bf16[2,64,1152]{2,1,0:T(8,128)(2,1)} %x_ref.1, bf16[2,64,1152]{2,1,0:T(8,128)(2,1)} %cot_ref.1, ...), custom_call_target="tpu_custom_call" | custom-call | tf_op jit(solution)/shard_map/blocks/pallas_call | solution.py:916
  246.5 1.9 convert_element_type.6
  248.3 0.0 copy-start.1
  248.3 1.9 copy-done.1
  250.2 0.1 slice.39
  250.3 0.4 copy.29
  250.7 1.6 copy.28
  252.3 0.0 copy-start
  252.3 1.0 slice.30
  253.3 0.1 reshape.40
  253.4 0.9 slice.29
  254.4 2.4 convolution_bitcast_fusion
  256.9 1.2 slice.40
  258.0 1.0 copy.30
  259.0 0.0 copy-done
  259.0 0.0 copy-start.4
  259.0 0.0 copy-start.3
  259.0 0.0 copy-start.2
  259.0 0.0 copy-start.5
  259.0 1.7 fusion.4
  260.7 0.0 copy-done.4
  260.7 0.6 slice_bitcast_fusion
  261.3 0.0 copy-done.3
  261.3 0.7 copy.36
  262.1 0.0 copy-done.2
  262.1 0.7 copy.37
  262.8 0.0 copy-done.5
  262.8 0.6 copy.38
  (2 shorter events, 0.0 us)
Async XLA Ops:
  248.3 1.9 copy-start.1
  252.3 6.7 %copy-start = (bf16[3,3,96,1152]{3,2,1,0:T(8,128)(2,1)S(1)}, bf16[3,3,96,1152]{3,2,1,0:T(8,128)(2,1)}, u32[]{:S(2)}) copy-start(bf16[3,3,96,1152]{3,2,1,0:T(8,128)(2,1)} %get-tuple-element.19) | copy-start | bytes 5971972
  259.0 1.7 copy-start.4
  259.0 2.3 copy-start.3
  259.0 3.0 %copy-start.2 = (bf16[2,64,1152]{2,1,0:T(8,128)(2,1)S(1)}, bf16[2,64,1152]{2,1,0:T(8,128)(2,1)}, u32[]{:S(2)}) copy-start(bf16[2,64,1152]{2,1,0:T(8,128)(2,1)} %get-tuple-element.18) | copy-start | bytes 884740
  259.0 3.8 %copy-start.5 = (f32[4,961]{1,0:T(4,128)S(1)}, f32[4,961]{1,0:T(4,128)}, u32[]{:S(2)}) copy-start(f32[4,961]{1,0:T(4,128)} %get-tuple-element.22) | copy-start | bytes 46132

commit v5 on v4

--- a/solution.py
+++ b/solution.py
@@ -64,7 +64,7 @@
     cfg,
     x_ref, cot_ref, wq_hbm, wt_hbm, wo_hbm, w1_hbm, w2_hbm, temb_ref, gain_ref, shift_ref, rel_ref, tab_ref,
     out_ref, ig_ref, tot_ref, tok_ref, emb_ref, gtab_ref, small_ref,
-    wq_ref, spare, wo_ref, w1_ref, w2_ref, tp_ref, tx_ref, chosen, tab, partial, arrived,
+    wq_ref, wo_ref, w1_ref, w2_ref, tp_ref, tx_ref, chosen, tab, partial, arrived,
     tiny_s, small_r,
     xin, gin, mid, gath, keep, rcv_c, rcv_y, snd_c, snd_y, bias, prob, qkv, att, act, dgel,
     xhat, inv, ymid, dqkv, dh, datt, acc, turned, far_att, act2, dh2, dqkv2, far_att2,
@@ -72,14 +72,15 @@
 ):
     count, rows, seq, heads, ring, chained = cfg
     half_rows = 2 * rows
+    wide = -(-wo_ref.shape[0] // 128) * 128
     width = x_ref.shape[-1]
     local = wo_ref.shape[0]
     grid = int(round(seq**0.5))
     windows = head_windows(heads, local)
     scale = (local // heads) ** (-0.5)
-    blocks = partial.shape[1] if chained else tot_ref.shape[1]
+    blocks = 4
     cut = width // blocks
-    pieces = partial.shape[2] if chained else 1
+    pieces = arrived.shape[2] if chained else 1
     slim = cut // pieces
     lanes = dqkv.shape[-1]
 
@@ -93,7 +94,7 @@
     there = 1 - here
     own = pl.ds(pl.multiple_of(t * rows, rows), rows)
 
-    wt_ref = partial.at[2, :3] if chained else spare
+    wt_ref = partial.at[2, : 3 * local, :]
 
     loads = [
         pltpu.make_async_copy(src, dst, load_s.at[n])
@@ -162,16 +163,16 @@
         low, high = part[:rows], part[rows:]
         snd_c[k % 2, i, which] = jnp.where(odd, low, high).astype(BF16)
         rs_copy(k, i, which).start()
-        keep[i, which] = jnp.where(odd, high, low)
+        keep[k % 2, i, which] = jnp.where(odd, high, low)
 
     def rs_pass(k, i):
         rs_copy(k, i, 0).wait_recv()
-        snd_y[k % 2, i] = (keep[i, 0] + rcv_c[k % 2, i, 0].astype(F32)).astype(BF16)
+        snd_y[k % 2, i] = (keep[k % 2, i, 0] + rcv_c[k % 2, i, 0].astype(F32)).astype(BF16)
         rs_copy(k, i, 2).start()
 
     def rs_take(k, i):
         rs_copy(k, i, 1).wait_recv()
-        near = keep[i, 1] + rcv_c[k % 2, i, 1].astype(F32)
+        near = keep[k % 2, i, 1] + rcv_c[k % 2, i, 1].astype(F32)
         rs_copy(k, i, 2).wait_recv()
         return near + rcv_y[k % 2, i].astype(F32)
 
@@ -214,6 +215,9 @@
     beyond = 3 * (2 - z)
     is_end = (z == 0) | (z == 3)
     is_mate = (z == 1) | (z == 2)
+
+    def rows_at(b, c):
+        return pl.ds(pl.multiple_of(b * cut + c * slim, slim), slim)
 
     def factor_copy(n):
         if n < 4:
@@ -250,14 +254,14 @@
 
     def cross_copy(w, slot, c):
         return pltpu.make_async_remote_copy(
-            src_ref=partial.at[w, (beyond, across)[slot], c], dst_ref=arrived.at[w, slot, c],
+            src_ref=partial.at[w, rows_at((beyond, across)[slot], c), :], dst_ref=arrived.at[w, slot, c],
             send_sem=ch_s.at[w, slot, c], recv_sem=ch_r.at[w, slot, c],
             device_id={"dp": across}, device_id_type=MESH,
         )
 
     def home_copy(w, c):
         return pltpu.make_async_remote_copy(
-            src_ref=partial.at[w, mate, c], dst_ref=arrived.at[w, 0, c],
+            src_ref=partial.at[w, rows_at(mate, c), :], dst_ref=arrived.at[w, 0, c],
             send_sem=ch_s.at[w, 2, c], recv_sem=ch_r.at[w, 0, c],
             device_id={"dp": mate}, device_id_type=MESH,
         )
@@ -279,19 +283,17 @@
             lax.fori_loop(0, blocks, whole, 0)
             return
 
-        def rows_at(b, c):
-            return pl.ds(pl.multiple_of(b * cut + c * slim, slim), slim)
-
         def alone(b):
             def one(c):
-                partial[w, b, c] = product(rows_at(b, c), 0).astype(BF16)
+                at = rows_at(b, c)
+                partial[w, at, :] = product(at, 0).astype(BF16)
 
             each_piece(one)
 
         def both(b, slot=None):
             def one(c):
                 at = rows_at(b, c)
-                partial[w, b, c] = (product(at, 0) + product(at, 1)).astype(BF16)
+                partial[w, at, :] = (product(at, 0) + product(at, 1)).astype(BF16)
                 if slot is not None:
                     cross_copy(w, slot, c).start()
 
@@ -318,8 +320,9 @@
         def _():
             def one(c):
                 cross_copy(w, 0, c).wait_recv()
-                partial[w, mate, c] = (
-                    partial[w, mate, c].astype(F32) + arrived[w, 0, c].astype(F32)
+                at = rows_at(mate, c)
+                partial[w, at, :] = (
+                    partial[w, at, :].astype(F32) + arrived[w, 0, c].astype(F32)
                 ).astype(BF16)
                 home_copy(w, c).start()
 
@@ -329,7 +332,7 @@
         def finish(slot, copy):
             def one(c):
                 copy(c).wait_recv()
-                tot_ref[w, c] = (partial[w, z, c].astype(F32) + arrived[w, slot, c].astype(F32)).astype(BF16)
+                tot_ref[w, c] = (partial[w, rows_at(z, c), :].astype(F32) + arrived[w, slot, c].astype(F32)).astype(BF16)
 
             each_piece(one)
 
@@ -392,6 +395,44 @@
         m1 = jnp.mean(dhat, axis=-1, keepdims=True)
         m2 = jnp.mean(dhat * hat, axis=-1, keepdims=True)
         return inv[which, i][:, :1] * (dhat - m1 - hat * m2)
+
+    def turn_qkv():
+        loads[1].wait()
+        for r in range(0, width, wide):
+            for c in range(3):
+                partial[1, r : r + wide, c * wide : c * wide + local] = wq_ref[
+                    c * local : (c + 1) * local, r : r + wide
+                ].T
+
+    def turn_weight(w, ref):
+        for r in range(0, width, wide):
+            partial[w, r : r + wide, : ref.shape[0]] = ref[:, r : r + wide].T
+
+    def lead(k, end, near):
+        def first(i):
+            end(i)
+
+            @pl.when(i == count - 1)
+            def _():
+                ag_pass(k, 0)
+
+            ag_near(k, i)
+            near(i)
+
+        each_image(first)
+
+    def follow(k, rest):
+        def second(i):
+            ag_rest(k, i)
+            rest(i)
+
+            @pl.when(i < count - 1)
+            def _():
+                ag_pass(k, i + 1)
+
+            rs_pass(k, i)
+
+        each_image(second)
 
     tiny_s[...] = jnp.zeros_like(tiny_s)
     tok_ref[z] = jnp.zeros_like(tok_ref[z])
@@ -460,7 +501,7 @@
         tp_ref[...] = jnp.zeros_like(tp_ref)
         emb = jnp.concatenate([temb_ref[...], jnp.zeros((16 - count, width), BF16)], axis=0)
         for c in range(3):
-            tp_ref[c] = mm_nt(emb, wt_ref[c].reshape(local, width))
+            tp_ref[c] = mm_nt(emb, partial[2, c * local : (c + 1) * local, :])
 
     @pl.when(s == 1)
     def _():
@@ -474,31 +515,42 @@
         each_image(spread_cot)
         turn(DMLP)
         give_factor(2)
-
-    each_image(take_input)
+        turn_qkv()
+        loads[2].wait()
+        turn_weight(2, wo_ref)
+        loads[3].wait()
+        turn_weight(0, w1_ref)
+        loads[4].wait()
+
+        def early(i):
+            dh[i] = mm_nt(gath[DMLP, i], w2_ref[...]).astype(BF16)
+
+        each_image(early)
 
     @pl.when(s == 0)
     def _():
+        each_image(take_input)
         tables()
-
-    loads[1].wait()
-    loads[2].wait()
+        turn_qkv()
+        for n in (2, 3, 4):
+            loads[n].wait()
 
     def project(i, half):
         a = gath[ATT, i, half_of(half), :]
+        part = mm(a, partial[1, :, : 2 * wide + local])
         for c in range(3):
-            part = mm_nt(a, wq_ref[c * local : (c + 1) * local, :])
-            qkv[c, i, half_of(half), :] = (part + tp_ref[c, pl.ds(i, 1), :]).astype(BF16)
-
-    def att_near(i):
-        ag_near(ATT, i)
-        project(i, here)
-
-    each_image(att_near)
+            qkv[c, i, half_of(half), :] = (
+                part[:, c * wide : c * wide + local] + tp_ref[c, pl.ds(i, 1), :]
+            ).astype(BF16)
+
+    def att_first(i):
+        @pl.when(s == 1)
+        def _():
+            take_input(i)
+
+    lead(ATT, att_first, lambda i: project(i, here))
 
     def att_rest(i):
-        ag_pass(ATT, i)
-        ag_rest(ATT, i)
         project(i, there)
         acc[0] = jnp.zeros_like(acc[0])
         for h, (lo, hi, start, stop) in enumerate(windows):
@@ -513,9 +565,8 @@
         far_att[i] = pltpu.roll(acc[0], far_att.shape[-1] - local, 1).astype(BF16)
         rs_give(ATT, i, 0, mm(att[i, half_of(there), :], wo_ref[...]))
         rs_give(ATT, i, 1, mm(att[i, half_of(here), :], wo_ref[...]))
-        rs_pass(ATT, i)
-
-    each_image(att_rest)
+
+    follow(ATT, att_rest)
 
     turn(ATT)
     give_factor(0, 7)
@@ -523,14 +574,10 @@
     def att_end(i):
         y = xin[i].astype(F32) + rs_take(ATT, i)
         ag_done(ATT, i)
+        rs_done(ATT, i)
         ymid[i] = y
         gath[MLP, i, own, :] = norm(y, 1, i)
         ag_start(MLP, i)
-
-    each_image(att_end)
-
-    loads[3].wait()
-    loads[4].wait()
 
     def mlp_half(i, half, which):
         a = gath[MLP, i, half_of(half), :]
@@ -542,25 +589,14 @@
         dgel[i, half_of(half), :] = slope.astype(BF16)
         rs_give(MLP, i, which, mm(act[i, half_of(half), :], w2_ref[...]))
 
-    def mlp_near(i):
-        ag_near(MLP, i)
-        mlp_half(i, here, 1)
-
-    each_image(mlp_near)
-
-    def mlp_rest(i):
-        ag_pass(MLP, i)
-        ag_rest(MLP, i)
-        mlp_half(i, there, 0)
-        rs_pass(MLP, i)
-
-    each_image(mlp_rest)
-
+    lead(MLP, att_end, lambda i: mlp_half(i, here, 1))
+    follow(MLP, lambda i: mlp_half(i, there, 0))
     turn(MLP)
     give_factor(1, 4)
 
     def mlp_end(i):
         mid[i] = (ymid[i] + rs_take(MLP, i)).astype(BF16)
+        rs_done(MLP, i)
 
         @pl.when(s == 0)
         def _():
@@ -570,8 +606,6 @@
         def _():
             out_ref[i] = mid[i]
             out_copy(i).start()
-
-    each_image(mlp_end)
 
     def take_grad(i):
         mid_copy(i).wait_send()
@@ -579,52 +613,60 @@
         gath[DMLP, i, own, :] = gin[i]
         ag_start(DMLP, i)
 
+    def dmlp_half(i, half, which):
+        @pl.when(s == 0)
+        def _():
+            dh[i, half_of(half), :] = mm(gath[DMLP, i, half_of(half), :], partial[1]).astype(BF16)
+
+        dact = dh[i, half_of(half), :].astype(F32)
+        dh[i, half_of(half), :] = (dact * dgel[i, half_of(half), :].astype(F32)).astype(BF16)
+        rs_give(DMLP, i, which, mm(dh[i, half_of(half), :], partial[0]))
+
     @pl.when(s == 0)
     def _():
-        each_image(take_grad)
+        each_image(mlp_end)
+        turn_weight(0, w1_ref)
+        turn_weight(1, w2_ref)
+        turn_weight(2, wo_ref)
+        lead(DMLP, take_grad, lambda i: dmlp_half(i, here, 1))
+
+    def dmlp_rest(i):
+        @pl.when(s == 0)
+        def _():
+            ag_rest(DMLP, i)
+
+            @pl.when(i == count - 1)
+            def _():
+                turn(DMLP)
+                give_factor(2)
+
+        dmlp_half(i, there, 0)
+
+        @pl.when(s == 1)
+        def _():
+            dmlp_half(i, here, 1)
+
+        @pl.when((s == 0) & (i < count - 1))
+        def _():
+            ag_pass(DMLP, i + 1)
+
+        rs_pass(DMLP, i)
+
+    each_image(dmlp_rest)
+    give_factor(5)
+
+    @pl.when(s == 0)
+    def _():
+        share_factor(ATT)
+        share_factor(MLP)
 
     @pl.when(s == 1)
     def _():
         def keep_cot(i):
             gin[i] = cot_ref[i]
+            mlp_end(i)
 
         each_image(keep_cot)
-
-    def dmlp_half(i, half, which):
-        dact = mm_nt(gath[DMLP, i, half_of(half), :], w2_ref[...])
-        dh[i, half_of(half), :] = (dact * dgel[i, half_of(half), :]).astype(BF16)
-        rs_give(DMLP, i, which, mm_nt(dh[i, half_of(half), :], w1_ref[...]))
-
-    def dmlp_near(i):
-        rs_done(ATT, i)
-
-        @pl.when(s == 0)
-        def _():
-            ag_near(DMLP, i)
-
-        dmlp_half(i, here, 1)
-
-    each_image(dmlp_near)
-
-    def dmlp_rest(i):
-        @pl.when(s == 0)
-        def _():
-            ag_pass(DMLP, i)
-            ag_rest(DMLP, i)
-
-        dmlp_half(i, there, 0)
-        rs_pass(DMLP, i)
-
-    each_image(dmlp_rest)
-
-    @pl.when(s == 0)
-    def _():
-        turn(DMLP)
-        give_factor(2)
-        share_factor(ATT)
-        share_factor(MLP)
-
-    give_factor(5)
 
     def dmlp_end(i):
         grad = gin[i].astype(F32) + norm_back(rs_take(DMLP, i), 1, i)
@@ -632,32 +674,25 @@
         gath[DATT % 3, i, own, :] = grad.astype(BF16)
         ag_start(DATT, i)
 
-    each_image(dmlp_end)
-
     def job_fc2():
         give_blocks(0, (2, 4), product(DMLP, act, act2))
 
     def job_fc1():
         give_blocks(1, (1, 5), product(MLP, dh, dh2))
+
+    def datt_part(i, half):
+        datt[i, half_of(half), :] = mm(
+            gath[DATT % 3, i, half_of(half), :], partial[2, :, :local]
+        ).astype(BF16)
+
+    lead(DATT, dmlp_end, lambda i: datt_part(i, here))
 
     @pl.when(s == 0)
     def _():
         share_factor(DMLP)
         job_fc2()
 
-    def datt_part(i, half):
-        datt[i, half_of(half), :] = mm_nt(gath[DATT % 3, i, half_of(half), :], wo_ref[...]).astype(BF16)
-
-    def datt_near(i):
-        rs_done(MLP, i)
-        ag_near(DATT, i)
-        datt_part(i, here)
-
-    each_image(datt_near)
-
     def datt_rest(i):
-        ag_pass(DATT, i)
-        ag_rest(DATT, i)
         datt_part(i, there)
         acc[...] = jnp.zeros_like(acc)
         for h, (lo, hi, start, stop) in enumerate(windows):
@@ -694,9 +729,8 @@
         tok_ref[z, pl.ds(i, 1), :lanes] = jnp.sum(dqkv[i].astype(F32), axis=0, keepdims=True)
         for which, half in ((0, there), (1, here)):
             rs_give(DATT, i, which, mm(dqkv[i, half_of(half), : 3 * local], wq_ref[...]))
-        rs_pass(DATT, i)
-
-    each_image(datt_rest)
+
+    follow(DATT, datt_rest)
 
     give_factor(6)
     turn(DATT)
@@ -835,9 +869,6 @@
     blocks = 4
     pieces = 3 if width // 4 % 48 == 0 else 1
     cut = width // blocks
-    chained = chained and local == width // 4
-    if chained:
-        wt = wt.reshape(3, pieces, local // pieces, width)
     padded = -(-local // 128) * 128
     lanes = -(-3 * local // 128) * 128
     dims = (count, rows, seq, heads, ring, chained)
@@ -855,7 +886,6 @@
     dma = pltpu.SemaphoreType.DMA
     scratch = [
         vm(wq.shape, BF16),
-        vm((16, 128) if chained else wt.shape, BF16),
         vm(wo.shape, BF16),
         vm(w1.shape, BF16),
         vm(w2.shape, BF16),
@@ -863,7 +893,7 @@
         vm((heads, int(round(seq**0.5)), 2 * seq), F32),
         vm((4 * seq, 4 * seq), BF16),
         vm((16, 4 * seq), F32),
-        vm((3, blocks, pieces, cut // pieces, width) if chained else (16, 128), BF16),
+        vm((3, width, width), BF16),
         vm((3, 2, pieces, cut // pieces, width) if chained else (16, 128), BF16),
         vm((2, 8, width), F32),
         vm((2, 3, 8, width), F32),
@@ -871,7 +901,7 @@
         vm((count, rows, width), BF16),
         vm((count, rows, width), BF16),
         vm((3, count, seq, width), BF16),
-        vm((count, 2, rows, width), F32),
+        vm((2, count, 2, rows, width), F32),
         vm((2, count, 2, rows, width), BF16),
         vm((2, count, rows, width), BF16),
         vm((2, count, 2, rows, width), BF16),
@@ -937,7 +967,7 @@
     cut = width // ring
     embedded = t_table[timesteps]
     wq = jnp.transpose(w_qkv[0], (1, 2, 0)).reshape(3 * local, width)
-    wt = jnp.transpose(w_time[0], (1, 2, 0))
+    wt = jnp.transpose(w_time[0], (1, 2, 0)).reshape(3 * local, width)
     output, in_grad, total, sums, emb, g_table, small = run_block(
         images, cotangent, wq, wt, w_out[0], w_fc1[0], w_fc2[0], embedded, norm_gain[0], norm_shift[0],
         rel_index, rel_table[0].T, ring,

time: 267 us -> 247 us (0.925)
  Pallas kernels: 242 us -> 222 us
    pallas_call x1, Pallas kernels: 242 us -> 222 us  [run_block(): pl.pallas_call(functools.partial(block_kernel, dims), out_shape=out_shape...]
where the time goes in v5:
time: 247 us; the launch traced here: 243 us
  Pallas kernels  222 us (90%)
  local copies, waits for them, and re-layouts  15.7 us (6%)
  other arithmetic  2.53 us (1%)
    pallas_call x1, Pallas kernels, run_block(): pl.pallas_call(functools.partial(block_kernel, dims), out_shape=out_shape...  222 us
    unnamed x18, local copies, waits for them, and re-layouts  6.9 us

profile of v5, /device:TPU:9, one launch (start us, length us, event | category | flops | bytes accessed | tf_op | source)
XLA Modules:
  0.0 243.0 jit_solution(576737142684317651)
XLA Ops:
  0.6 0.7 compare_select_fusion
  1.3 3.1 %gather_fusion = bf16[2,1152]{1,0:T(2,128)(2,1)} fusion(bf16[1000,1152]{1,0:T(8,128)(2,1)} %param.15, s32[1024]{0:T(1024)S(1)} %pad_clamp_fusion), kind=kCustom, calls=%fused_computation | custom fusion | bytes 9224 | tf_op jit(solution)/shard_map/gather | solution.py:968
  4.4 221.7 %blocks.1 = (bf16[2,64,1152]{2,1,0:T(8,128)(2,1)}, bf16[2,64,1152]{2,1,0:T(8,128)(2,1)}, bf16[3,3,96,1152]{3,2,1,0:T(8,128)(2,1)}, f32[4,8,1152]{2,1,0:T(8,128)}...) custom-call(bf16[2,64,1152]{2,1,0:T(8,128)(2,1)} %x_ref.1, bf16[2,64,1152]{2,1,0:T(8,128)(2,1)} %cot_ref.1, ...), custom_call_target="tpu_custom_call" | custom-call | tf_op jit(solution)/shard_map/blocks/pallas_call | solution.py:946
  226.1 1.9 convert_element_type.6
  227.9 0.0 copy-start.1
  228.0 1.9 copy-done.1
  229.8 0.1 slice.39
  229.9 0.4 copy.29
  230.3 1.6 copy.28
  231.9 0.0 copy-start
  231.9 1.0 slice.30
  233.0 0.1 reshape.40
  233.1 0.9 slice.29
  234.0 2.4 %convolution_bitcast_fusion = f32[1,288,3,288]{3,1,2,0:T(8,128)} fusion(f32[8,3,288]{2,1,0:T(4,128)S(1)} %reshape.40, f32[8,1152]{1,0:T(8,128)S(1)} %reshape.39, s32[]{:T(128)S(6)} %select_n.7), kind=kOutput, calls=%fused_computation.1 | convolution fusion | flops 23887872 | bytes 1056772 | tf_op jit(solution)/shard_map/id,icj->dcj/dot_general | solution.py:986
  236.5 1.2 slice.40
  237.7 1.0 copy.30
  238.6 0.0 copy-done
  238.6 0.0 copy-start.4
  238.6 0.0 copy-start.3
  238.6 0.0 copy-start.2
  238.6 0.0 copy-start.5
  238.7 1.7 fusion.4
  240.4 0.0 copy-done.4
  240.4 0.6 slice_bitcast_fusion
  241.0 0.0 copy-done.3
  241.0 0.7 copy.36
  241.7 0.0 copy-done.2
  241.7 0.7 copy.37
  242.4 0.0 copy-done.5
  242.4 0.6 copy.38
  (2 shorter events, 0.0 us)
Async XLA Ops:
  227.9 1.9 copy-start.1
  231.9 6.7 %copy-start = (bf16[3,3,96,1152]{3,2,1,0:T(8,128)(2,1)S(1)}, bf16[3,3,96,1152]{3,2,1,0:T(8,128)(2,1)}, u32[]{:S(2)}) copy-start(bf16[3,3,96,1152]{3,2,1,0:T(8,128)(2,1)} %get-tuple-element.19) | copy-start | bytes 5971972
  238.6 1.7 copy-start.4
  238.6 2.3 copy-start.3
  238.6 3.0 %copy-start.2 = (bf16[2,64,1152]{2,1,0:T(8,128)(2,1)S(1)}, bf16[2,64,1152]{2,1,0:T(8,128)(2,1)}, u32[]{:S(2)}) copy-start(bf16[2,64,1152]{2,1,0:T(8,128)(2,1)} %get-tuple-element.18) | copy-start | bytes 884740
  238.6 3.8 %copy-start.5 = (f32[4,961]{1,0:T(4,128)S(1)}, f32[4,961]{1,0:T(4,128)}, u32[]{:S(2)}) copy-start(f32[4,961]{1,0:T(4,128)} %get-tuple-element.22) | copy-start | bytes 46132
